TPU v7x, 32 devices: a whole 2x2x4 slice. The times are simulated.
32 devices in a mesh: section: 4 (over y, x), expert: 4 (over z), pair: 2 (over core).
Axes of the slice: x: 2, y: 2, z: 4, core: 2. Of those that a mesh axis runs over, the one named last changes fastest.
Arguments:
- initial_state: bfloat16 [2048, 2048], P(('section', 'expert')), may hold values from -6 to 6
- prelude: bfloat16 [2048, 2048], P(('section', 'expert')), may hold values from -6 to 6
- inject_gain: float32 [2048], replicated, may hold values from 0.1 to 1.9
- norm_gain: float32 [2048], replicated, may hold values from 0.1 to 1.9
- router: bfloat16 [2048, 64], replicated, may hold values from -0.125 to 0.125
- gate_w: bfloat16 [64, 2048, 1024], P('expert', 'section', 'pair'), may hold values from -0.125 to 0.125
- up_w: bfloat16 [64, 2048, 1024], P('expert', 'section', 'pair'), may hold values from -0.125 to 0.125
- down_w: bfloat16 [64, 1024, 2048], P('expert', 'pair', 'section'), may hold values from -0.1875 to 0.1875
- routes: int32 [1, 2048, 8], P(None, ('section', 'expert')), may hold values from 0 to 63, all different within a row; in each aligned block of 128 rows (0 to 127, 128 to 255, ..., all dimensions but the last counted through in order) at most 18 rows name the same one
Outputs:
- final_state: bfloat16 [2048, 2048], P(('section', 'expert'), 'pair')
Inputs may be any that keep to these rules, and one draw needn't show every extreme that they name: `routes`: each row names 8 different experts. Within the 128 rows of one device in one pass (aligned blocks of the token dimension), no expert is named more than 18 times, a bound that some block reaches.
All inputs are finite; a program needn't handle non-finite values.
Results may differ from a plain program's by a relative error of at most 0.0029.
Values may be sent and summed in bfloat16 or wider, within the bound.
A program may use at most 192 MiB of HBM per device.

v0:
```python
import jax
import jax.numpy as jnp
from jax import lax
from jax.sharding import PartitionSpec as P

TOPK = 8
CAP = 18


def on_device(initial_state, prelude, inject_gain, norm_gain, router, gate_w, up_w, down_w, routes):
    gate_full, up_full, down_full = (
        lax.all_gather(gate_w, "section", axis=1, tiled=True),
        lax.all_gather(up_w, "section", axis=1, tiled=True),
        lax.all_gather(down_w, "section", axis=2, tiled=True),
    )
    paired_w = jnp.concatenate([gate_full, up_full], axis=2)
    local_count = gate_full.shape[0]
    half_width = gate_full.shape[2]
    tok_count, model_width = initial_state.shape
    experts_all = router.shape[1]
    pair_count = lax.axis_size("pair")
    pair_pos = lax.axis_index("pair")
    part_width = model_width // pair_count
    hidden_state = initial_state.astype(jnp.float32)
    prelude_f = prelude.astype(jnp.float32)
    token_ids = jnp.broadcast_to(
        jnp.arange(tok_count, dtype=jnp.int32)[:, None], (tok_count, TOPK)
    ).reshape(-1)
    expert_range = jnp.arange(experts_all, dtype=jnp.int32)
    mixed_state = hidden_state + prelude_f * inject_gain
    inv_rms = lax.rsqrt(jnp.mean(mixed_state * mixed_state, axis=-1, keepdims=True) + 1e-06)
    normed = (mixed_state * inv_rms * norm_gain).astype(jnp.bfloat16)
    logits = jnp.dot(normed, router, preferred_element_type=jnp.float32)
    router_prob = jax.nn.sigmoid(logits)
    chosen = routes[0]
    onehot_k = (chosen[:, :, None] == expert_range).astype(jnp.float32)
    picked = jnp.sum(onehot_k * router_prob[:, None, :], axis=-1)
    gate_vals = picked / jnp.sum(picked, axis=1, keepdims=True)
    flat_ids = chosen.reshape(-1)
    onehot = (flat_ids[:, None] == expert_range).astype(jnp.int32)
    before = jnp.cumsum(onehot, axis=0) - onehot
    slot_rank = jnp.sum(before * onehot, axis=-1)
    slot_ids = flat_ids * CAP + slot_rank
    source_rows = jnp.full((experts_all * CAP,), tok_count, jnp.int32).at[slot_ids].set(token_ids)
    padded_rows = jnp.concatenate([normed, jnp.zeros((1, model_width), jnp.bfloat16)], axis=0)
    outgoing = padded_rows[source_rows].reshape(experts_all, CAP, padded_rows.shape[1])
    received = lax.all_to_all(outgoing, "expert", split_axis=0, concat_axis=0, tiled=True)
    slot_count = received.shape[1]
    grouped = received.reshape(-1, local_count, slot_count, model_width)
    gate_up = jnp.einsum("sekd,edh->sekh", grouped, paired_w, preferred_element_type=jnp.float32)
    inner_act = (jax.nn.silu(gate_up[..., :half_width]) * gate_up[..., half_width:]).astype(
        jnp.bfloat16
    )
    partial_out = jnp.einsum(
        "sekh,ehd->sekd", inner_act, down_full, preferred_element_type=jnp.float32
    ).astype(jnp.bfloat16)
    lead = partial_out.shape[0]
    pieces = jnp.moveaxis(
        partial_out.reshape(lead, local_count, slot_count, pair_count, part_width), 3, 0
    )
    arrived = lax.all_to_all(pieces, "pair", split_axis=0, concat_axis=0, tiled=True)
    summed = jnp.sum(arrived.astype(jnp.float32), axis=0).astype(jnp.bfloat16)
    returned_rows = lax.all_to_all(
        summed.reshape(-1, slot_count, summed.shape[-1]),
        "expert",
        split_axis=0,
        concat_axis=0,
        tiled=True,
    )
    back_width = returned_rows.shape[-1]
    flat_back = returned_rows.reshape(experts_all * CAP, back_width)
    taken_rows = flat_back[slot_ids].reshape(tok_count, TOPK, back_width)
    moe_out = jnp.sum(gate_vals[:, :, None] * taken_rows.astype(jnp.float32), axis=1)
    hidden_state = (
        lax.dynamic_slice_in_dim(mixed_state, pair_pos * part_width, part_width, 1) + moe_out
    )
    return hidden_state.astype(jnp.bfloat16)


def solution(mesh):
    placed = (
        P(("section", "expert"), None),
        P(("section", "expert"), None),
        P(),
        P(),
        P(),
        P("expert", "section", "pair"),
        P("expert", "section", "pair"),
        P("expert", "pair", "section"),
        P(None, ("section", "expert"), None),
    )
    return jax.shard_map(
        on_device,
        mesh=mesh,
        in_specs=placed,
        out_specs=P(("section", "expert"), "pair"),
        check_vma=False,
    )
```

profile of v0, /device:TPU:0, one launch (start us, length us, event | category | flops | bytes accessed | tf_op | source)
XLA Modules:
  0.0 1054.1 jit_solution(8598139006022780238)
XLA Ops:
  6.5 0.7 all-gather.4.cloned.1.call-update
  7.3 0.7 all-gather.6.cloned.1.call-update
  8.1 0.7 all-gather.8.cloned.1.call-update
  9.1 18.0 %reduce-window.6 = s32[64,8,128]{2,1,0:T(8,128)S(1)} reduce-window(s32[64,8,128]{2,1,0:T(8,128)S(1)} %fusion.19, s32[]{:T(128)} %constant.13.clone.1), window={size=1x1x128 pad=0_0x0_0x127_0}, to_apply=%region_3.0 | reduce-window | flops 8323072 | bytes 524292 | tf_op jit(solution)/shard_map/reduce-window
  27.1 0.1 slice.20
  27.3 0.1 copy.66
  27.9 0.3 multiply_reduce_fusion
  28.2 1.0 copy-done.1
  29.2 0.2 multiply_convert_fusion
  29.4 0.1 broadcast_add_fusion
  29.6 4.3 scatter_custom_fusion
  34.0 5.9 gather_fusion
  39.9 7.6 reshape.98
  47.5 146.5 %all_to_all.15 = bf16[64,18,2048]{2,1,0:T(8,128)(2,1)} all-to-all(bf16[64,18,2048]{2,1,0:T(8,128)(2,1)} %reshape.98), channel_id=1, replica_groups=mesh['section'=4,'expert'=4,'pair'=2] {'expert'}, dimensions={0} | all-to-all | bytes 9437184 | tf_op jit(solution)/shard_map/all_to_all | solution.py:47
  194.0 115.3 %all-gather.4.cloned.1.call-done = bf16[16,2048,512]{2,1,0:T(8,128)(2,1)} async-done(((bf16[16,512,512]{2,1,0:T(8,128)(2,1)}), bf16[16,2048,512]{2,1,0:T(8,128)(2,1)}) %all-gather.4.cloned.1.call-update) | async-done | bytes 33554448 | tf_op jit(solution)/shard_map/all_gather | solution.py:12
  309.2 299.1 %all-gather.6.cloned.1.call-done = bf16[16,2048,512]{2,1,0:T(8,128)(2,1)} async-done(((bf16[16,512,512]{2,1,0:T(8,128)(2,1)}), bf16[16,2048,512]{2,1,0:T(8,128)(2,1)}) %all-gather.6.cloned.1.call-update) | async-done | bytes 33554448 | tf_op jit(solution)/shard_map/all_gather | solution.py:13
  608.3 33.2 %fusion.8 = f32[4,16,18,1024]{3,2,0,1:T(8,128)} fusion(bf16[4,16,18,2048]{3,2,1,0:T(8,128)(2,1)} %bitcast.52, bf16[16,2048,512]{2,1,0:T(8,128)(2,1)} %all-gather.6.cloned.1.call-done, bf16[16,2048,512]{2,1,0:T(8,128)(2,1)} %all-gather.4.cloned.1.call-done), kind=kOutput, calls=%fused_computation.13 | convolution fusion | flops 4966055936 | bytes 76546048 | tf_op jit(solution)/shard_map/sekd,edh->sekh/dot_general | solution.py:50
  641.5 265.8 %all-gather.8.cloned.1.call-done = bf16[16,512,2048]{2,1,0:T(8,128)(2,1)} async-done(((bf16[16,512,512]{2,1,0:T(8,128)(2,1)}), bf16[16,512,2048]{2,1,0:T(8,128)(2,1)}) %all-gather.8.cloned.1.call-update) | async-done | bytes 33554448 | tf_op jit(solution)/shard_map/all_gather | solution.py:14
  907.3 18.0 %convert_bitcast_fusion = bf16[4,16,18,2048]{3,2,0,1:T(8,128)(2,1)} fusion(bf16[16,512,2048]{2,1,0:T(8,128)(2,1)} %all-gather.8.cloned.1.call-done, f32[4,16,18,1024]{3,2,0,1:T(8,128)} %fusion.8), kind=kOutput, calls=%fused_computation.8 | convolution fusion | flops 2421817344 | bytes 42991616 | tf_op jit(solution)/shard_map/sekh,ehd->sekd/dot_general | solution.py:54
  925.3 12.1 %reshape.131 = bf16[4,16,18,2,1024]{4,3,2,0,1:T(2,128)(2,1)} reshape(bf16[4,16,18,2048]{3,2,0,1:T(8,128)(2,1)} %convert_bitcast_fusion) | data formatting | bytes 9437184 | tf_op jit(solution)/shard_map/reshape | solution.py:59
  937.5 4.9 copy.71
  942.4 8.6 all_to_all.16
  951.0 4.0 reduce_sum.64
  955.1 0.4 copy.73
  955.5 3.1 copy.74
  958.5 4.6 all-to-all-start.2
  963.2 0.3 fusion.15
  963.7 70.8 %all-to-all-done.2 = bf16[64,18,1024]{2,1,0:T(8,128)(2,1)} async-done(((bf16[64,18,1024]{2,1,0:T(8,128)(2,1)}), bf16[64,18,1024]{2,1,0:T(8,128)(2,1)}, u32[]{:S(2)}, u32[]{:S(2)}) %all-to-all-start.2) | async-done | bytes 2359328 | tf_op jit(solution)/shard_map/all_to_all | solution.py:63
  1034.6 2.9 reshape.102
  1037.5 5.4 gather_fusion.1
  1042.9 2.9 fusion.6
  1045.8 1.8 add_convert_fusion
  (38 shorter events, 1.2 us)
Async XLA Ops:
  6.5 956.7 %copy-start = (bf16[2048,64]{0,1:T(8,128)(2,1)S(1)}, bf16[2048,64]{0,1:T(8,128)(2,1)}, u32[]{:S(2)}) copy-start(bf16[2048,64]{0,1:T(8,128)(2,1)} %param.13) | copy-start | bytes 786436
  6.5 302.7 %all-gather.4.cloned.1.call-start = ((), (), s32[]{:S(2)}) async-start(), calls=%async_computation.3 | async-start | bytes 41943040 | tf_op jit(solution)/shard_map/all_gather | solution.py:12
  7.3 1.5 copy-start.4
  7.3 601.1 %all-gather.6.cloned.1.call-start = ((), (), s32[]{:S(2)}) async-start(), calls=%async_computation.4 | async-start | bytes 41943040 | tf_op jit(solution)/shard_map/all_gather | solution.py:13
  8.0 19.8 %copy-start.2 = (bf16[128,2048]{1,0:T(8,128)(2,1)S(1)}, bf16[128,2048]{1,0:T(8,128)(2,1)}, u32[]{:S(2)}) copy-start(bf16[128,2048]{1,0:T(8,128)(2,1)} %param.10) | copy-start | bytes 1572868
  8.0 19.8 %copy-start.3 = (bf16[128,2048]{1,0:T(8,128)(2,1)S(1)}, bf16[128,2048]{1,0:T(8,128)(2,1)}, u32[]{:S(2)}) copy-start(bf16[128,2048]{1,0:T(8,128)(2,1)} %param.9) | copy-start | bytes 1572868
  8.0 19.8 %copy-start.5 = (f32[2048]{0:T(1024)S(1)}, f32[2048]{0:T(1024)}, u32[]{:S(2)}) copy-start(f32[2048]{0:T(1024)} %param.11) | copy-start | bytes 24580
  8.0 21.1 %copy-start.6 = (f32[2048]{0:T(1024)S(1)}, f32[2048]{0:T(1024)}, u32[]{:S(2)}) copy-start(f32[2048]{0:T(1024)} %param.12) | copy-start | bytes 24580
  8.1 899.2 %all-gather.8.cloned.1.call-start = ((), (), s32[]{:S(2)}) async-start(), calls=%async_computation.5 | async-start | bytes 41943040 | tf_op jit(solution)/shard_map/all_gather | solution.py:14
  28.2 1.0 copy-start.1
  958.5 76.0 %all-to-all-start.2 = ((bf16[64,18,1024]{2,1,0:T(8,128)(2,1)}), bf16[64,18,1024]{2,1,0:T(8,128)(2,1)}, u32[]{:S(2)}, u32[]{:S(2)}) async-start(bf16[64,18,1024]{2,1,0:T(8,128)(2,1)} %copy.74), calls=%async_computation.2 | async-start | bytes 6291456 | tf_op jit(solution)/shard_map/all_to_all | solution.py:63
Sparse Core Ops, SparseCore 0:
  9.2 299.9 all-gather.3
  311.1 297.2 all-gather.5
  610.2 297.0 all-gather.7
where the time goes:
time: 1060 us; the launch traced here: 1050 us
  waiting for transfers between devices  753 us (71%)
  blocking collectives  155 us (15%)
  matrix products  51.5 us (5%)
  local copies, waits for them, and re-layouts  48.7 us (5%)
  other arithmetic  27.6 us (3%)
  between operations  13.4 us (1%)
    all_gather x1, waiting for transfers between devices, on_device(): lax.all_gather(up_w, 'section', axis=1, tiled=True)  299 us
    all_gather x1, waiting for transfers between devices, on_device(): lax.all_gather(down_w, 'section', axis=2, tiled=True)  266 us
    all_to_all x1, blocking collectives, on_device(): lax.all_to_all(outgoing, 'expert', split_axis=0, concat_axis=0, tiled=True)  146 us
    all_gather x1, waiting for transfers between devices, on_device(): lax.all_gather(gate_w, 'section', axis=1, tiled=True)  115 us
    all_to_all x1, waiting for transfers between devices, on_device(): lax.all_to_all(summed.reshape(-1, slot_count, summed.shape[-1]), 'expert'...  70.8 us
    dot_general x1, matrix products, on_device(): jnp.einsum('sekd,edh->sekh', grouped, paired_w, preferred_element_type=jn...  33.2 us
  transfers between devices with their start and end apart: 4, of which 4 were waited for; matrix products, arithmetic and copies ran while one was open for 7% of the time, Pallas kernels for 0%

commit v1 on v0

--- a/solution.py
+++ b/solution.py
@@ -7,7 +7,7 @@
 CAP = 18
 
 
-def on_device(initial_state, prelude, inject_gain, norm_gain, router, gate_w, up_w, down_w, routes):
+def gather_weights(initial_state, prelude, inject_gain, norm_gain, router, gate_w, up_w, down_w, routes):
     gate_full, up_full, down_full = (
         lax.all_gather(gate_w, "section", axis=1, tiled=True),
         lax.all_gather(up_w, "section", axis=1, tiled=True),
@@ -37,9 +37,11 @@
     picked = jnp.sum(onehot_k * router_prob[:, None, :], axis=-1)
     gate_vals = picked / jnp.sum(picked, axis=1, keepdims=True)
     flat_ids = chosen.reshape(-1)
-    onehot = (flat_ids[:, None] == expert_range).astype(jnp.int32)
-    before = jnp.cumsum(onehot, axis=0) - onehot
-    slot_rank = jnp.sum(before * onehot, axis=-1)
+    onehot = (flat_ids[:, None] == expert_range).astype(jnp.bfloat16)
+    order = jnp.arange(flat_ids.shape[0], dtype=jnp.int32)
+    earlier = (order[:, None] > order[None, :]).astype(jnp.bfloat16)
+    before = jnp.dot(earlier, onehot, preferred_element_type=jnp.float32)
+    slot_rank = jnp.sum(before * onehot.astype(jnp.float32), axis=-1).astype(jnp.int32)
     slot_ids = flat_ids * CAP + slot_rank
     source_rows = jnp.full((experts_all * CAP,), tok_count, jnp.int32).at[slot_ids].set(token_ids)
     padded_rows = jnp.concatenate([normed, jnp.zeros((1, model_width), jnp.bfloat16)], axis=0)
@@ -77,6 +79,95 @@
     return hidden_state.astype(jnp.bfloat16)
 
 
+def move_tokens(initial_state, prelude, inject_gain, norm_gain, router, gate_w, up_w, down_w, routes):
+    sections, zs, pairs = (lax.axis_size(a) for a in ("section", "expert", "pair"))
+    pair_pos = lax.axis_index("pair")
+    local_count, depth, _ = gate_w.shape
+    tok_count, model_width = initial_state.shape
+    experts_all = router.shape[1]
+    part_width = model_width // pairs
+    slots = CAP * zs
+    sec_toks = zs * tok_count
+
+    all_routes = lax.all_gather(routes[0], ("section", "expert"), axis=0, tiled=True)
+    all_routes = all_routes.reshape(sections, sec_toks, TOPK)
+
+    mixed = initial_state.astype(jnp.float32) + prelude.astype(jnp.float32) * inject_gain
+    inv_rms = lax.rsqrt(jnp.mean(mixed * mixed, axis=-1, keepdims=True) + 1e-06)
+    normed = (mixed * inv_rms * norm_gain).astype(jnp.bfloat16)
+
+    half_toks = tok_count // pairs
+    mine = lax.dynamic_slice_in_dim(normed, pair_pos * half_toks, half_toks, 0)
+    sliced = lax.all_to_all(mine, "section", split_axis=1, concat_axis=0, tiled=True)
+    rows = lax.all_gather(sliced, ("expert", "pair"), axis=0, tiled=False)
+    rows = rows.reshape(zs, pairs, sections, half_toks, depth)
+    rows = rows.transpose(2, 0, 1, 3, 4).reshape(sections, sec_toks, depth)
+
+    logits = jnp.dot(normed, router, preferred_element_type=jnp.float32)
+    prob = jax.nn.sigmoid(logits)
+    onehot_k = (routes[0][:, :, None] == jnp.arange(experts_all, dtype=jnp.int32)).astype(jnp.float32)
+    picked = jnp.sum(onehot_k * prob[:, None, :], axis=-1)
+    gates = picked / jnp.sum(picked, axis=1, keepdims=True)
+    all_gates = lax.all_gather(gates, ("section", "expert"), axis=0, tiled=True)
+    all_gates = all_gates.reshape(sections, sec_toks, TOPK)
+
+    first = lax.axis_index("expert") * local_count
+    own = first + jnp.arange(local_count, dtype=jnp.int32)
+    hits = all_routes[:, None, :, :] == own[None, :, None, None]
+    member = jnp.any(hits, axis=-1)
+    member_gate = jnp.sum(jnp.where(hits, all_gates[:, None, :, :], 0.0), axis=-1)
+    order = jnp.arange(sec_toks, dtype=jnp.int32)
+    earlier = (order[:, None] < order[None, :]).astype(jnp.bfloat16)
+    rank = jnp.einsum(
+        "seu,ut->set", member.astype(jnp.bfloat16), earlier, preferred_element_type=jnp.float32
+    )
+    place = jnp.where(member, rank, -1.0).astype(jnp.int32)
+    at_slot = place[:, :, None, :] == jnp.arange(slots, dtype=jnp.int32)[:, None]
+    dispatch = at_slot.astype(jnp.bfloat16)
+    combine = jnp.where(at_slot, member_gate[:, :, None, :], 0.0).astype(jnp.bfloat16)
+
+    grouped = jnp.einsum(
+        "sect,std->secd", dispatch, rows, preferred_element_type=jnp.float32
+    ).astype(jnp.bfloat16)
+
+    def product(weight):
+        part = jnp.einsum(
+            "secd,edh->sech", grouped, weight, preferred_element_type=jnp.float32
+        ).astype(jnp.bfloat16)
+        parts = lax.all_to_all(part, "section", split_axis=0, concat_axis=0, tiled=True)
+        return jnp.sum(parts.astype(jnp.float32), axis=0)
+
+    act = (jax.nn.silu(product(gate_w)) * product(up_w)).astype(jnp.bfloat16)
+    all_act = lax.all_gather(act, "section", axis=0, tiled=False)
+    outs = jnp.einsum(
+        "sech,ehd->secd", all_act, down_w, preferred_element_type=jnp.float32
+    ).astype(jnp.bfloat16)
+    moe = jnp.einsum("sect,secd->std", combine, outs, preferred_element_type=jnp.float32)
+
+    fine = depth // pairs
+    moe = moe.astype(jnp.bfloat16).reshape(sections, zs, tok_count, pairs, fine)
+    moe = lax.all_to_all(moe.transpose(3, 1, 0, 2, 4), "pair", split_axis=0, concat_axis=0, tiled=True)
+    moe = jnp.sum(moe.astype(jnp.float32), axis=0).astype(jnp.bfloat16)
+    moe = lax.all_to_all(moe, "expert", split_axis=0, concat_axis=0, tiled=True)
+    moe = jnp.sum(moe.astype(jnp.float32), axis=0).astype(jnp.bfloat16)
+    moe = lax.all_to_all(moe, "section", split_axis=0, concat_axis=0, tiled=True)
+    moe = moe.reshape(pairs, sections // pairs, tok_count, fine)
+    moe = lax.all_to_all(moe, "pair", split_axis=0, concat_axis=0, tiled=True)
+    moe = moe.transpose(2, 1, 0, 3).reshape(tok_count, part_width)
+    state = lax.dynamic_slice_in_dim(mixed, pair_pos * part_width, part_width, 1)
+    return (state + moe.astype(jnp.float32)).astype(jnp.bfloat16)
+
+
+def on_device(initial_state, prelude, inject_gain, norm_gain, router, gate_w, up_w, down_w, routes):
+    sections, zs, pairs = (lax.axis_size(a) for a in ("section", "expert", "pair"))
+    slot_bytes = 2 * sections * gate_w.shape[0] * CAP * zs * zs * initial_state.shape[0]
+    fits = slot_bytes <= 16 * 2**20 and sections % pairs == 0 and initial_state.shape[0] % pairs == 0
+    plan = move_tokens if fits else gather_weights
+    return plan(
+        initial_state, prelude, inject_gain, norm_gain, router, gate_w, up_w, down_w, routes
+    )
+
+
 def solution(mesh):
     placed = (
         P(("section", "expert"), None),

time: 1060 us -> 319 us (0.30)
  waiting for transfers between devices: 753 us -> 107 us
  local copies, waits for them, and re-layouts: 48.7 us -> 14.2 us
  blocking collectives: 155 us -> 128 us
  matrix products: 51.5 us -> 29.3 us
  other arithmetic: 27.6 us -> 13.1 us
    all_gather x3 -> x2, waiting for transfers between devices: 680 us -> 17.5 us  [the longest x1 17.4 us: move_tokens(): all_act = lax.all_gather(act, 'section', axis=0, tiled=False)]
    all_to_all x2 -> x4, blocking collectives: 155 us -> 50.6 us  [the longest x1 30.5 us: move_tokens(): moe = lax.all_to_all(moe, 'expert', split_axis=0, concat_axis=0, tiled=True)]
    all_gather x0 -> x2, blocking collectives: none -> 77.3 us  [the longest x1 40.7 us: move_tokens(): lax.all_gather(routes[0], ('section', 'expert'), axis=0, tiled=True)]
    reshape x5 -> x2, local copies, waits for them, and re-layouts: 25.8 us -> 2.93 us  [move_tokens(): moe = moe.astype(jnp.bfloat16).reshape(sections, zs, tok_count, pairs, fine)]
    dot_general x3 -> x6, matrix products: 51.5 us -> 29.3 us  [the longest x2 12.9 us: product(): jnp.einsum('secd,edh->sech', grouped, weight, preferred_element_type=jnp....]
    all_to_all x1 -> x3, waiting for transfers between devices: 70.8 us -> 89.5 us  [the longest x2 84.2 us: product(): lax.all_to_all(part, 'section', split_axis=0, concat_axis=0, tiled=True)]
    another operation x3 -> x0, other arithmetic: 18.2 us -> none
    gather x2 -> x0, local copies, waits for them, and re-layouts: 11.3 us -> none  [the longest x1 5.95 us: on_device(): padded_rows[source_rows].reshape(experts_all, CAP, padded_rows.shape[1])]
  transfers between devices with their start and end apart: 4 -> 5, of which waited for: 4 -> 4; matrix products, arithmetic and copies ran while one was open for 7% -> 5% of each run, Pallas kernels for 0% -> 0%
where the time goes in v1:
time: 319 us
  blocking collectives  128 us (40%)
  waiting for transfers between devices  107 us (34%)
  matrix products  29.3 us (9%)
  local copies, waits for them, and re-layouts  14.2 us (4%)
  between operations  13.7 us (4%)
  starting transfers between devices  13.4 us (4%)
  other arithmetic  13.1 us (4%)
    all_to_all x2, waiting for transfers between devices, product(): lax.all_to_all(part, 'section', split_axis=0, concat_axis=0, tiled=True)  84.2 us
    all_gather x1, blocking collectives, move_tokens(): lax.all_gather(routes[0], ('section', 'expert'), axis=0, tiled=True)  40.7 us
    all_gather x1, blocking collectives, move_tokens(): all_gates = lax.all_gather(gates, ('section', 'expert'), axis=0, tiled=True)  36.7 us
    all_to_all x1, blocking collectives, move_tokens(): moe = lax.all_to_all(moe, 'expert', split_axis=0, concat_axis=0, tiled=True)  30.5 us
    all_gather x1, waiting for transfers between devices, move_tokens(): all_act = lax.all_gather(act, 'section', axis=0, tiled=False)  17.4 us
    dot_general x2, matrix products, product(): jnp.einsum('secd,edh->sech', grouped, weight, preferred_element_type=jnp....  12.9 us
    dot_general x1, matrix products, move_tokens(): jnp.einsum('sect,secd->std', combine, outs, preferred_element_type=jnp.fl...  11.6 us
    all_to_all x1, blocking collectives, move_tokens(): lax.all_to_all(mine, 'section', split_axis=1, concat_axis=0, tiled=True)  10.8 us
  transfers between devices with their start and end apart: 5, of which 4 were waited for; matrix products, arithmetic and copies ran while one was open for 5% of the time, Pallas kernels for 0%

profile of v1, /device:TPU:0, one launch (start us, length us, event | category | flops | bytes accessed | tf_op | source)
XLA Modules:
  0.0 318.5 jit_solution(10053471636520122315)
XLA Ops:
  6.5 1.4 copy.66
  7.9 1.3 copy.67
  9.2 1.1 multiply_reduce_fusion
  10.3 1.1 multiply_convert_fusion
  11.8 10.8 %all_to_all.46 = bf16[64,4,512]{2,0,1:T(8,128)(2,1)} all-to-all(bf16[64,4,512]{2,0,1:T(8,128)(2,1)S(1)} %copy.69), channel_id=1, replica_groups=mesh['section'=4,'expert'=4,'pair'=2] {'section'}, dimensions={1} | all-to-all | bytes 524288 | tf_op jit(solution)/shard_map/all_to_all | solution.py:101
  22.6 40.7 %all-gather = s32[1,2048,8]{1,2,0:T(8,128)S(1)} all-gather(s32[1,128,8]{1,2,0:T(8,128)S(1)} %copy-done.3), channel_id=2, replica_groups=mesh['section'=4,'expert'=4,'pair'=2] {'section','expert'}, dimensions={1}, use_global_device_ids=true | all-gather | bytes 69632 | tf_op jit(solution)/shard_map/all_gather | solution.py:92
  63.3 0.4 compare_reduce_fusion
  64.0 1.9 copy.70
  65.9 4.3 %fusion.24 = bf16[4,16,72,512]{3,2,1,0:T(8,128)(2,1)} fusion(bf16[4,512,512,1]{2,1,3,0:T(8,128)(2,1)S(1)} %bitcast.85, s32[4,16,512]{2,1,0:T(8,128)S(1)} %fusion.35), kind=kOutput, calls=%fused_computation.23 | convolution fusion | flops 2420637696 | bytes 6946816 | tf_op jit(solution)/shard_map/sect,std->secd/dot_general | solution.py:129
  70.2 5.5 %convert_bitcast_fusion = bf16[4,16,72,512]{3,2,0,1:T(8,128)(2,1)S(1)} fusion(bf16[16,512,512]{2,1,0:T(8,128)(2,1)S(1)} %bitcast.94, bf16[4,16,72,512]{3,2,1,0:T(8,128)(2,1)} %fusion.24), kind=kOutput, calls=%fused_computation.14 | convolution fusion | flops 2418278400 | bytes 17825792 | tf_op jit(solution)/shard_map/secd,edh->sech/dot_general | solution.py:134
  75.8 2.5 copy.74
  78.3 4.9 %all-to-all-start.2 = ((bf16[4,16,72,512]{3,2,1,0:T(8,128)(2,1)}), bf16[4,16,72,512]{3,2,1,0:T(8,128)(2,1)}, u32[]{:S(2)}, u32[]{:S(2)}) async-start(bf16[4,16,72,512]{3,2,1,0:T(8,128)(2,1)} %copy.74), calls=%async_computation.2 | async-start | bytes 9437184 | tf_op jit(solution)/shard_map/all_to_all | solution.py:137
  83.2 7.4 %convert_bitcast_fusion.1 = bf16[4,16,72,512]{3,2,0,1:T(8,128)(2,1)S(1)} fusion(bf16[16,512,512]{2,1,0:T(8,128)(2,1)} %param.14, bf16[4,16,72,512]{3,2,1,0:T(8,128)(2,1)} %fusion.24), kind=kOutput, calls=%fused_computation.15 | convolution fusion | flops 2418278400 | bytes 17825792 | tf_op jit(solution)/shard_map/secd,edh->sech/dot_general | solution.py:134
  90.7 2.6 copy.72
  93.3 35.0 %all-to-all-done.2 = bf16[4,16,72,512]{3,2,1,0:T(8,128)(2,1)} async-done(((bf16[4,16,72,512]{3,2,1,0:T(8,128)(2,1)}), bf16[4,16,72,512]{3,2,1,0:T(8,128)(2,1)}, u32[]{:S(2)}, u32[]{:S(2)}) %all-to-all-start.2) | async-done | bytes 4718624 | tf_op jit(solution)/shard_map/all_to_all | solution.py:137
  128.3 5.0 %all-to-all-start.1 = ((bf16[4,16,72,512]{3,2,1,0:T(8,128)(2,1)}), bf16[4,16,72,512]{3,2,1,0:T(8,128)(2,1)}, u32[]{:S(2)}, u32[]{:S(2)}) async-start(bf16[4,16,72,512]{3,2,1,0:T(8,128)(2,1)} %copy.72), calls=%async_computation.1 | async-start | bytes 9437184 | tf_op jit(solution)/shard_map/all_to_all | solution.py:137
  133.4 3.3 %convert_reduce_fusion = f32[16,72,512]{2,1,0:T(8,128)S(1)} fusion(bf16[4,16,72,512]{3,2,1,0:T(8,128)(2,1)} %all-to-all-done.2), kind=kLoop, calls=%fused_computation | loop fusion | flops 4128768 | bytes 7077888 | tf_op jit(solution)/shard_map/reduce_sum | solution.py:138
  136.6 49.1 %all-to-all-done.1 = bf16[4,16,72,512]{3,2,1,0:T(8,128)(2,1)} async-done(((bf16[4,16,72,512]{3,2,1,0:T(8,128)(2,1)}), bf16[4,16,72,512]{3,2,1,0:T(8,128)(2,1)}, u32[]{:S(2)}, u32[]{:S(2)}) %all-to-all-start.1) | async-done | bytes 4718624 | tf_op jit(solution)/shard_map/all_to_all | solution.py:137
  185.8 3.3 %convert_reduce_fusion.1 = f32[16,72,512]{2,1,0:T(8,128)S(1)} fusion(bf16[4,16,72,512]{3,2,1,0:T(8,128)(2,1)} %all-to-all-done.1), kind=kLoop, calls=%fused_computation.1 | loop fusion | flops 4128768 | bytes 7077888 | tf_op jit(solution)/shard_map/reduce_sum | solution.py:138
  189.1 1.8 fusion.25
  191.3 36.7 %all_gather.17 = f32[2048,8]{0,1:T(8,128)S(1)} all-gather(f32[128,8]{0,1:T(8,128)S(1)} %broadcast_divide_fusion), channel_id=1, replica_groups=mesh['section'=4,'expert'=4,'pair'=2] {'section','expert'}, dimensions={0}, use_global_device_ids=true | all-gather | bytes 69632 | tf_op jit(solution)/shard_map/all_gather | solution.py:111
  228.3 17.4 %all-gather.6.cloned.1.call-done = bf16[4,16,72,512]{3,2,1,0:T(8,128)(2,1)} async-done(((bf16[1,16,72,512]{3,2,1,0:T(8,128)(2,1)}), bf16[4,16,72,512]{3,2,1,0:T(8,128)(2,1)}) %all-gather.6.cloned.1.call-update) | async-done | bytes 4718608 | tf_op jit(solution)/shard_map/all_gather | solution.py:141
  245.8 11.6 %bitcast_convert_fusion = bf16[4,512,512]{2,1,0:T(8,128)(2,1)} fusion(bf16[4,16,512]{2,1,0:T(8,128)(2,1)S(1)} %fusion.39, s32[4,16,512]{2,1,0:T(8,128)S(1)} %fusion.35, bf16[4,16,72,512]{3,2,1,0:T(8,128)(2,1)} %all-gather.6.cloned.1.call-done, bf16[16,512,512]{2,1,0:T(8,128)(2,1)} %param.16), kind=kOutput, calls=%fused_computation.20 | convolution fusion | flops 4839964672 | bytes 15400960 | tf_op jit(solution)/shard_map/sect,secd->std/dot_general | solution.py:145
  257.3 2.5 reshape.71
  260.3 5.4 %all_to_all.47 = bf16[2,4,4,128,256]{4,3,1,2,0:T(8,128)(2,1)S(1)} all-to-all(bf16[2,4,4,128,256]{4,3,1,2,0:T(8,128)(2,1)S(1)} %bitcast.83), channel_id=1, replica_groups=mesh['section'=4,'expert'=4,'pair'=2] {'pair'}, dimensions={0} | all-to-all | bytes 4194304 | tf_op jit(solution)/shard_map/all_to_all | solution.py:149
  265.7 0.7 reduce_sum.90
  266.5 30.5 %all_to_all.48 = bf16[4,4,128,256]{3,2,1,0:T(8,128)(2,1)S(1)} all-to-all(bf16[4,4,128,256]{3,2,1,0:T(8,128)(2,1)S(1)} %copy.77), channel_id=1, replica_groups=mesh['section'=4,'expert'=4,'pair'=2] {'expert'}, dimensions={0} | all-to-all | bytes 2097152 | tf_op jit(solution)/shard_map/all_to_all | solution.py:151
  296.9 0.9 reduce_sum.91
  297.8 3.4 %all-to-all-start.5 = ((bf16[4,128,256]{2,1,0:T(8,128)(2,1)}), bf16[4,128,256]{2,1,0:T(8,128)(2,1)S(1)}, u32[]{:S(2)}, u32[]{:S(2)}) async-start(bf16[4,128,256]{2,1,0:T(8,128)(2,1)} %reduce_sum.91), calls=%async_computation.5 | async-start | bytes 524288 | tf_op jit(solution)/shard_map/all_to_all | solution.py:153
  301.3 5.3 %all-to-all-done.5 = bf16[4,128,256]{2,1,0:T(8,128)(2,1)S(1)} async-done(((bf16[4,128,256]{2,1,0:T(8,128)(2,1)}), bf16[4,128,256]{2,1,0:T(8,128)(2,1)S(1)}, u32[]{:S(2)}, u32[]{:S(2)}) %all-to-all-start.5) | async-done | bytes 262176 | tf_op jit(solution)/shard_map/all_to_all | solution.py:153
  306.6 3.9 %all_to_all.49 = bf16[2,2,128,256]{3,2,1,0:T(8,128)(2,1)S(1)} all-to-all(bf16[2,2,128,256]{3,2,1,0:T(8,128)(2,1)S(1)} %bitcast.88), channel_id=1, replica_groups=mesh['section'=4,'expert'=4,'pair'=2] {'pair'}, dimensions={0} | all-to-all | bytes 524288 | tf_op jit(solution)/shard_map/all_to_all | solution.py:155
  310.8 0.9 copy.79
  (32 shorter events, 2.2 us)
Async XLA Ops:
  6.5 184.4 %copy-start = (bf16[2048,64]{0,1:T(8,128)(2,1)S(1)}, bf16[2048,64]{0,1:T(8,128)(2,1)}, u32[]{:S(2)}) copy-start(bf16[2048,64]{0,1:T(8,128)(2,1)} %param.13) | copy-start | bytes 786436
  6.5 16.1 %copy-start.3 = (s32[1,128,8]{1,2,0:T(8,128)S(1)}, s32[1,128,8]{1,2,0:T(8,128)}, u32[]{:S(2)}) copy-start(s32[1,128,8]{1,2,0:T(8,128)} %param.17) | copy-start | bytes 12292
  6.5 57.4 %all-gather.4.cloned.1.call-start = ((), (), s32[]{:S(2)}) async-start(), calls=%async_computation.7 | async-start | bytes 2359296 | tf_op jit(solution)/shard_map/all_gather | solution.py:102
  10.3 59.9 %copy-start.1 = (f32[128,2048]{0,1:T(8,128)}, f32[128,2048]{0,1:T(8,128)S(1)}, u32[]{:S(2)}) copy-start(f32[128,2048]{0,1:T(8,128)S(1)} %get-tuple-element.8) | copy-start | bytes 3145732
  64.0 6.3 %slice-start = ((s8[8388608]{0:T(1024)(128)(4,1)}), s8[4194304]{0:T(1024)(128)(4,1)S(1)}, s32[]{:S(2)}) async-start(s8[8388608]{0:T(1024)(128)(4,1)} %bitcast.93), calls=%async_computation.9 | async-start | bytes 8388608
  65.9 4.4 %slice-start.1 = ((s8[8388608]{0:T(1024)(128)(4,1)}), s8[4194304]{0:T(1024)(128)(4,1)S(1)}, s32[]{:S(2)}) async-start(s8[8388608]{0:T(1024)(128)(4,1)} %bitcast.93), calls=%async_computation.10 | async-start | bytes 8388608
  78.3 50.0 %all-to-all-start.2 = ((bf16[4,16,72,512]{3,2,1,0:T(8,128)(2,1)}), bf16[4,16,72,512]{3,2,1,0:T(8,128)(2,1)}, u32[]{:S(2)}, u32[]{:S(2)}) async-start(bf16[4,16,72,512]{3,2,1,0:T(8,128)(2,1)} %copy.74), calls=%async_computation.2 | async-start | bytes 9437184 | tf_op jit(solution)/shard_map/all_to_all | solution.py:137
  128.3 57.4 %all-to-all-start.1 = ((bf16[4,16,72,512]{3,2,1,0:T(8,128)(2,1)}), bf16[4,16,72,512]{3,2,1,0:T(8,128)(2,1)}, u32[]{:S(2)}, u32[]{:S(2)}) async-start(bf16[4,16,72,512]{3,2,1,0:T(8,128)(2,1)} %copy.72), calls=%async_computation.1 | async-start | bytes 9437184 | tf_op jit(solution)/shard_map/all_to_all | solution.py:137
  133.3 112.4 %all-gather.6.cloned.1.call-start = ((), (), s32[]{:S(2)}) async-start(), calls=%async_computation.8 | async-start | bytes 5898240 | tf_op jit(solution)/shard_map/all_gather | solution.py:141
  266.4 44.4 %copy-start.2 = (f32[128,2048]{0,1:T(8,128)S(1)}, f32[128,2048]{0,1:T(8,128)}, u32[]{:S(2)}) copy-start(f32[128,2048]{0,1:T(8,128)} %copy-done.1) | copy-start | bytes 3145732
  297.8 8.8 %all-to-all-start.5 = ((bf16[4,128,256]{2,1,0:T(8,128)(2,1)}), bf16[4,128,256]{2,1,0:T(8,128)(2,1)S(1)}, u32[]{:S(2)}, u32[]{:S(2)}) async-start(bf16[4,128,256]{2,1,0:T(8,128)(2,1)} %reduce_sum.91), calls=%async_computation.5 | async-start | bytes 524288 | tf_op jit(solution)/shard_map/all_to_all | solution.py:153
Sparse Core Ops, SparseCore 0:
  22.7 29.4 all-gather.3
  191.0 54.6 all-gather.5

commit v2 on v1

--- a/solution.py
+++ b/solution.py
@@ -81,38 +81,60 @@
 
 def move_tokens(initial_state, prelude, inject_gain, norm_gain, router, gate_w, up_w, down_w, routes):
     sections, zs, pairs = (lax.axis_size(a) for a in ("section", "expert", "pair"))
-    pair_pos = lax.axis_index("pair")
+    me, z, pair_pos = (lax.axis_index(a) for a in ("section", "expert", "pair"))
     local_count, depth, _ = gate_w.shape
     tok_count, model_width = initial_state.shape
     experts_all = router.shape[1]
     part_width = model_width // pairs
     slots = CAP * zs
     sec_toks = zs * tok_count
-
-    all_routes = lax.all_gather(routes[0], ("section", "expert"), axis=0, tiled=True)
-    all_routes = all_routes.reshape(sections, sec_toks, TOPK)
+    half_toks = tok_count // pairs
+    first_core = pair_pos == 0
+
+    def to_section(x, j):
+        return lax.ppermute(x, "section", [(s, s ^ j) for s in range(sections)])
+
+    def to_lower(x, k):
+        return lax.ppermute(x, "expert", [(i, (i - k) % zs) for i in range(zs)])
+
+    def to_upper(x, k):
+        return lax.ppermute(x, "expert", [(i, (i + k) % zs) for i in range(zs)])
+
+    def to_other_core(x):
+        return lax.ppermute(x, "pair", [(0, 1), (1, 0)])
 
     mixed = initial_state.astype(jnp.float32) + prelude.astype(jnp.float32) * inject_gain
     inv_rms = lax.rsqrt(jnp.mean(mixed * mixed, axis=-1, keepdims=True) + 1e-06)
     normed = (mixed * inv_rms * norm_gain).astype(jnp.bfloat16)
 
-    half_toks = tok_count // pairs
     mine = lax.dynamic_slice_in_dim(normed, pair_pos * half_toks, half_toks, 0)
-    sliced = lax.all_to_all(mine, "section", split_axis=1, concat_axis=0, tiled=True)
-    rows = lax.all_gather(sliced, ("expert", "pair"), axis=0, tiled=False)
-    rows = rows.reshape(zs, pairs, sections, half_toks, depth)
-    rows = rows.transpose(2, 0, 1, 3, 4).reshape(sections, sec_toks, depth)
+    sliced = []
+    for j in range(sections):
+        piece = lax.dynamic_slice_in_dim(mine, (me ^ j) * depth, depth, 1)
+        sliced.append(piece if j == 0 else to_section(piece, j))
+    sliced = jnp.stack(sliced)
+    half = jnp.stack([sliced if k == 0 else to_upper(sliced, k) for k in range(zs)], axis=1)
+    other = to_other_core(half)
+    rows = jnp.where(
+        first_core, jnp.stack([half, other], axis=2), jnp.stack([other, half], axis=2)
+    ).reshape(sections, sec_toks, depth)
 
     logits = jnp.dot(normed, router, preferred_element_type=jnp.float32)
     prob = jax.nn.sigmoid(logits)
     onehot_k = (routes[0][:, :, None] == jnp.arange(experts_all, dtype=jnp.int32)).astype(jnp.float32)
     picked = jnp.sum(onehot_k * prob[:, None, :], axis=-1)
     gates = picked / jnp.sum(picked, axis=1, keepdims=True)
-    all_gates = lax.all_gather(gates, ("section", "expert"), axis=0, tiled=True)
-    all_gates = all_gates.reshape(sections, sec_toks, TOPK)
-
-    first = lax.axis_index("expert") * local_count
-    own = first + jnp.arange(local_count, dtype=jnp.int32)
+    table = jnp.concatenate([routes[0].astype(jnp.float32), gates], axis=1)
+    table = lax.all_gather(table, ("section", "expert"), axis=0, tiled=False)
+    table = table.reshape(sections, zs, tok_count, 2 * TOPK)
+    table = jnp.stack([lax.dynamic_index_in_dim(table, me ^ j, 0, False) for j in range(sections)])
+    table = jnp.stack(
+        [lax.dynamic_index_in_dim(table, lax.rem(z + zs - k, zs), 1, False) for k in range(zs)], axis=1
+    )
+    table = table.reshape(sections, sec_toks, 2 * TOPK)
+    all_routes, all_gates = table[..., :TOPK].astype(jnp.int32), table[..., TOPK:]
+
+    own = z * local_count + jnp.arange(local_count, dtype=jnp.int32)
     hits = all_routes[:, None, :, :] == own[None, :, None, None]
     member = jnp.any(hits, axis=-1)
     member_gate = jnp.sum(jnp.where(hits, all_gates[:, None, :, :], 0.0), axis=-1)
@@ -130,30 +152,55 @@
         "sect,std->secd", dispatch, rows, preferred_element_type=jnp.float32
     ).astype(jnp.bfloat16)
 
-    def product(weight):
-        part = jnp.einsum(
-            "secd,edh->sech", grouped, weight, preferred_element_type=jnp.float32
+    def product(a, b, weight):
+        x = jnp.concatenate([grouped[a], grouped[b]], axis=1)
+        return jnp.einsum("ecd,edh->ech", x, weight, preferred_element_type=jnp.float32)
+
+    def summed(weight, near, far):
+        got = to_section(product(near, 3, weight).astype(jnp.bfloat16), near)
+        both = product(0, far, weight) + got.astype(jnp.float32)
+        got = to_section(both[:, slots:].astype(jnp.bfloat16), far)
+        return both[:, :slots] + got.astype(jnp.float32)
+
+    act = (jax.nn.silu(summed(gate_w, 1, 2)) * summed(up_w, 2, 1)).astype(jnp.bfloat16)
+
+    act1, act2 = to_section(act, 1), to_section(act, 2)
+    cut = local_count // 2
+    act3 = (to_section(act1[:cut], 2), to_section(act2[cut:], 1))
+
+    def gated_sum(j, a, lo, hi):
+        out = jnp.einsum(
+            "ech,ehd->ecd", a, down_w[lo:hi], preferred_element_type=jnp.float32
         ).astype(jnp.bfloat16)
-        parts = lax.all_to_all(part, "section", split_axis=0, concat_axis=0, tiled=True)
-        return jnp.sum(parts.astype(jnp.float32), axis=0)
-
-    act = (jax.nn.silu(product(gate_w)) * product(up_w)).astype(jnp.bfloat16)
-    all_act = lax.all_gather(act, "section", axis=0, tiled=False)
-    outs = jnp.einsum(
-        "sech,ehd->secd", all_act, down_w, preferred_element_type=jnp.float32
-    ).astype(jnp.bfloat16)
-    moe = jnp.einsum("sect,secd->std", combine, outs, preferred_element_type=jnp.float32)
-
-    fine = depth // pairs
-    moe = moe.astype(jnp.bfloat16).reshape(sections, zs, tok_count, pairs, fine)
-    moe = lax.all_to_all(moe.transpose(3, 1, 0, 2, 4), "pair", split_axis=0, concat_axis=0, tiled=True)
-    moe = jnp.sum(moe.astype(jnp.float32), axis=0).astype(jnp.bfloat16)
-    moe = lax.all_to_all(moe, "expert", split_axis=0, concat_axis=0, tiled=True)
-    moe = jnp.sum(moe.astype(jnp.float32), axis=0).astype(jnp.bfloat16)
-    moe = lax.all_to_all(moe, "section", split_axis=0, concat_axis=0, tiled=True)
-    moe = moe.reshape(pairs, sections // pairs, tok_count, fine)
-    moe = lax.all_to_all(moe, "pair", split_axis=0, concat_axis=0, tiled=True)
-    moe = moe.transpose(2, 1, 0, 3).reshape(tok_count, part_width)
+        return jnp.einsum(
+            "ect,ecd->td", combine[j, lo:hi], out, preferred_element_type=jnp.float32
+        )
+
+    def deliver(low, high, shift):
+        low, high = (b.astype(jnp.bfloat16).reshape(zs, tok_count, depth) for b in (low, high))
+        got = to_other_core(jnp.where(first_core, high, low))
+        kept = jnp.where(first_core, low, high)
+        both = (kept.astype(jnp.float32) + got.astype(jnp.float32)).astype(jnp.bfloat16)
+        total = both[0].astype(jnp.float32)
+        for k in range(1, zs):
+            total = total + to_lower(both[k], k).astype(jnp.float32)
+        moves = []
+        for s in range(sections):
+            for p in range(pairs):
+                moves.append((s * pairs + p, (s ^ (shift + 2 * p)) * pairs + s // 2))
+        return lax.ppermute(total.astype(jnp.bfloat16), ("section", "pair"), moves)
+
+    block0 = gated_sum(0, act, 0, local_count)
+    block1 = gated_sum(1, act1, 0, local_count)
+    block2 = gated_sum(2, act2, 0, local_count)
+    same = deliver(block0, block2, 0)
+    block3 = gated_sum(3, act3[0], 0, cut) + gated_sum(3, act3[1], cut, local_count)
+    unlike = deliver(block1, block3, 1)
+    moe = jnp.where(
+        me % 2 == 0,
+        jnp.concatenate([same, unlike], axis=1),
+        jnp.concatenate([unlike, same], axis=1),
+    )
     state = lax.dynamic_slice_in_dim(mixed, pair_pos * part_width, part_width, 1)
     return (state + moe.astype(jnp.float32)).astype(jnp.bfloat16)
 
@@ -161,7 +208,7 @@
 def on_device(initial_state, prelude, inject_gain, norm_gain, router, gate_w, up_w, down_w, routes):
     sections, zs, pairs = (lax.axis_size(a) for a in ("section", "expert", "pair"))
     slot_bytes = 2 * sections * gate_w.shape[0] * CAP * zs * zs * initial_state.shape[0]
-    fits = slot_bytes <= 16 * 2**20 and sections % pairs == 0 and initial_state.shape[0] % pairs == 0
+    fits = slot_bytes <= 16 * 2**20 and sections == 4 and pairs == 2
     plan = move_tokens if fits else gather_weights
     return plan(
         initial_state, prelude, inject_gain, norm_gain, router, gate_w, up_w, down_w, routes

time: 319 us -> 257 us (0.81)
  blocking collectives: 128 us -> 47.7 us
  starting transfers between devices: 13.4 us -> 29.7 us
  matrix products: 29.3 us -> 44.3 us
  between operations: 13.7 us -> 0.45 us
  local copies, waits for them, and re-layouts: 14.2 us -> 5.76 us
  waiting for transfers between devices: 107 us -> 114 us
    ppermute x0 -> x25, waiting for transfers between devices: none -> 114 us  [the longest x11 89.3 us: to_section(): return lax.ppermute(x, 'section', [(s, s ^ j) for s in range(sections)])]
    all_to_all x3 -> x0, waiting for transfers between devices: 89.5 us -> none  [the longest x2 84.2 us: product(): lax.all_to_all(part, 'section', split_axis=0, concat_axis=0, tiled=True)]
    all_to_all x4 -> x0, blocking collectives: 50.6 us -> none  [the longest x1 30.5 us: move_tokens(): moe = lax.all_to_all(moe, 'expert', split_axis=0, concat_axis=0, tiled=True)]
    ppermute x0 -> x25, starting transfers between devices: none -> 29.7 us  [the longest x11 14.3 us: to_section(): return lax.ppermute(x, 'section', [(s, s ^ j) for s in range(sections)])]
    all_gather x2 -> x1, blocking collectives: 77.3 us -> 47.7 us  [move_tokens(): table = lax.all_gather(table, ('section', 'expert'), axis=0, tiled=False)]
    all_gather x2 -> x0, waiting for transfers between devices: 17.5 us -> none  [the longest x1 17.4 us: move_tokens(): all_act = lax.all_gather(act, 'section', axis=0, tiled=False)]
    dot_general x3 -> x9, matrix products: 24.5 us -> 40.8 us  [the longest x5 30.6 us: gated_sum(): jnp.einsum('ect,ecd->td', combine[j, lo:hi], out, preferred_element_type=...]
    all_to_all x3 -> x0, starting transfers between devices: 13.3 us -> none  [the longest x2 9.91 us: product(): lax.all_to_all(part, 'section', split_axis=0, concat_axis=0, tiled=True)]
  transfers between devices with their start and end apart: 5 -> 25, of which waited for: 4 -> 12; matrix products, arithmetic and copies ran while one was open for 5% -> 19% of each run, Pallas kernels for 0% -> 0%
where the time goes in v2:
time: 257 us
  waiting for transfers between devices  114 us (44%)
  blocking collectives  47.7 us (19%)
  matrix products  44.3 us (17%)
  starting transfers between devices  29.7 us (12%)
  other arithmetic  15 us (6%)
  local copies, waits for them, and re-layouts  5.76 us (2%)
    ppermute x11, waiting for transfers between devices, to_section(): return lax.ppermute(x, 'section', [(s, s ^ j) for s in range(sections)])  89.3 us
    all_gather x1, blocking collectives, move_tokens(): table = lax.all_gather(table, ('section', 'expert'), axis=0, tiled=False)  47.7 us
    dot_general x5, matrix products, gated_sum(): jnp.einsum('ect,ecd->td', combine[j, lo:hi], out, preferred_element_type=...  30.6 us
    ppermute x6, waiting for transfers between devices, to_lower(): return lax.ppermute(x, 'expert', [(i, (i - k) % zs) for i in range(zs)])  17.1 us
    ppermute x11, starting transfers between devices, to_section(): return lax.ppermute(x, 'section', [(s, s ^ j) for s in range(sections)])  14.3 us
    dot_general x4, matrix products, product(): jnp.einsum('ecd,edh->ech', x, weight, preferred_element_type=jnp.float32)  10.2 us
    ppermute x6, starting transfers between devices, to_lower(): return lax.ppermute(x, 'expert', [(i, (i - k) % zs) for i in range(zs)])  6.97 us
    ppermute x3, starting transfers between devices, to_upper(): return lax.ppermute(x, 'expert', [(i, (i + k) % zs) for i in range(zs)])  6.48 us
  transfers between devices with their start and end apart: 25, of which 12 were waited for; matrix products, arithmetic and copies ran while one was open for 19% of the time, Pallas kernels for 0%

profile of v2, /device:TPU:0, one launch (start us, length us, event | category | flops | bytes accessed | tf_op | source)
XLA Modules:
  0.0 256.6 jit_solution(18252549249983603383)
XLA Ops:
  2.6 4.0 %collective-permute-start.2 = (bf16[64,512]{1,0:T(8,128)(2,1)S(1)}, bf16[64,512]{1,0:T(8,128)(2,1)S(1)}, u32[]{:S(2)}, u32[]{:S(2)}) collective-permute-start(bf16[64,512]{1,0:T(8,128)(2,1)S(1)} %get-tuple-element.26), channel_id=1, source_target_pairs={{0,24},{8,16},{16,8},{24,0},{1,25},{9,17},{17,9},{25,1},{2,26},{10... | collective-permute-start | bytes 196616 | tf_op jit(solution)/shard_map/ppermute | solution.py:95
  8.8 2.0 collective-permute-done.1
  11.4 2.7 %collective-permute-start.4 = (bf16[4,64,512]{2,1,0:T(8,128)(2,1)S(1)}, bf16[4,64,512]{2,1,0:T(8,128)(2,1)}, u32[]{:S(2)}, u32[]{:S(2)}) collective-permute-start(bf16[4,64,512]{2,1,0:T(8,128)(2,1)S(1)} %get-tuple-element.30), channel_id=1, source_target_pairs={{0,4},{2,6},{4,0},{6,2},{1,5},{3,7},{5,1},{7,3},{8,12},{10,14},{12... | collective-permute-start | bytes 786440 | tf_op jit(solution)/shard_map/ppermute | solution.py:101
  14.1 1.6 collective-permute-start.3
  15.6 2.2 collective-permute-start.5
  17.9 47.7 %all-gather = f32[2048,16]{0,1:T(8,128)S(1)} all-gather(f32[128,16]{0,1:T(8,128)S(1)} %pad_maximum_fusion.20), channel_id=2, replica_groups=mesh['section'=4,'expert'=4,'pair'=2] {'section','expert'}, dimensions={0}, use_global_device_ids=true | all-gather | bytes 139264 | tf_op jit(solution)/shard_map/all_gather | solution.py:128
  69.0 1.7 collective-permute-done.6
  70.7 1.9 maximum_select_fusion
  72.7 3.0 %fusion.6 = bf16[4,16,72,512]{3,2,1,0:T(8,128)(2,1)S(1)} fusion(bf16[4,512,512,1]{2,1,3,0:T(8,128)(2,1)S(1)} %bitcast.128, s32[4,16,512]{2,1,0:T(8,128)S(1)} %fusion.30), kind=kOutput, calls=%fused_computation.10 | convolution fusion | flops 2420637696 | bytes 6946816 | tf_op jit(solution)/shard_map/sect,std->secd/dot_general | solution.py:151
  76.1 2.8 %fusion.17 = bf16[16,144,512]{2,1,0:T(8,128)(2,1)} fusion(bf16[16,512,512]{2,1,0:T(8,128)(2,1)S(1)} %bitcast.125, bf16[16,72,512]{2,1,0:T(8,128)(2,1)S(1)} %get-tuple-element.10, bf16[16,72,512]{2,1,0:T(8,128)(2,1)S(1)} %get-tuple-element.11), kind=kOutput, calls=%fused_computation.30 | convolution fusion | flops 1213857792 | bytes 13107200 | tf_op jit(solution)/shard_map/ecd,edh->ech/dot_general | solution.py:157
  80.5 2.8 %fusion.18 = bf16[16,144,512]{2,1,0:T(8,128)(2,1)} fusion(bf16[16,512,512]{2,1,0:T(8,128)(2,1)S(1)} %bitcast.127, bf16[16,72,512]{2,1,0:T(8,128)(2,1)S(1)} %get-tuple-element.10, bf16[16,72,512]{2,1,0:T(8,128)(2,1)S(1)} %get-tuple-element.9), kind=kOutput, calls=%fused_computation.31 | convolution fusion | flops 1213857792 | bytes 13107200 | tf_op jit(solution)/shard_map/ecd,edh->ech/dot_general | solution.py:157
  83.3 49.2 %collective-permute-done.9 = bf16[16,144,512]{2,1,0:T(8,128)(2,1)S(1)} collective-permute-done((bf16[16,144,512]{2,1,0:T(8,128)(2,1)}, bf16[16,144,512]{2,1,0:T(8,128)(2,1)S(1)}, u32[]{:S(2)}, u32[]{:S(2)}) %collective-permute-start.9) | collective-permute-done | bytes 2359328 | tf_op jit(solution)/shard_map/ppermute | solution.py:95
  133.9 3.2 %convert_add_fusion = f32[16,144,512]{2,1,0:T(8,128)S(1)} fusion(bf16[16,144,512]{2,1,0:T(8,128)(2,1)} %copy-done.2, bf16[16,512,512]{2,1,0:T(8,128)(2,1)S(1)} %bitcast.125, bf16[16,72,512]{2,1,0:T(8,128)(2,1)S(1)} %get-tuple-element.12, bf16[16,72,512]{2,1,0:T(8,128)(2,1)S(1)} %get-tuple-element.9), kind=kOutput, calls=%fused_computation.3 | convolution fusion | flops 1215037440 | bytes 17825792 | tf_op jit(solution)/shard_map/ecd,edh->ech/dot_general | solution.py:157
  138.9 1.6 collective-permute-start.8
  140.9 23.5 %collective-permute-done.10 = bf16[16,72,512]{2,1,0:T(8,128)(2,1)S(1)} collective-permute-done((bf16[16,72,512]{2,1,0:T(8,128)(2,1)S(1)}, bf16[16,72,512]{2,1,0:T(8,128)(2,1)S(1)}, u32[]{:S(2)}, u32[]{:S(2)}) %collective-permute-start.10) | collective-permute-done | bytes 1179680 | tf_op jit(solution)/shard_map/ppermute | solution.py:95
  164.5 1.7 collective-permute-done.8
  167.1 1.8 collective-permute-start.17
  170.4 5.0 %select_convert_fusion = bf16[4,16,72,512]{3,2,1,0:T(8,128)(2,1)} fusion(bf16[4,16,512]{2,1,0:T(8,128)(2,1)S(1)} %fusion.34, s32[4,16,512]{2,1,0:T(8,128)S(1)} %fusion.30), kind=kLoop, calls=%fused_computation | loop fusion | flops 4718592 | bytes 4915200 | tf_op jit(solution)/shard_map/convert_element_type | solution.py:149
  175.4 6.9 %fusion.26 = bf16[512,512]{1,0:T(8,128)(2,1)} fusion(bf16[4,16,72,512]{3,2,1,0:T(8,128)(2,1)} %select_convert_fusion, bf16[16,72,512]{2,1,0:T(8,128)(2,1)S(1)} %fusion.12, bf16[16,512,512]{2,1,0:T(8,128)(2,1)} %param.16), kind=kOutput, calls=%fused_computation.45 | convolution fusion | flops 1208811520 | bytes 11272192 | tf_op jit(solution)/shard_map/ect,ecd->td/dot_general | solution.py:175
  182.3 11.2 %collective-permute-done.17 = bf16[16,72,512]{2,1,0:T(8,128)(2,1)} collective-permute-done((bf16[16,72,512]{2,1,0:T(8,128)(2,1)S(1)}, bf16[16,72,512]{2,1,0:T(8,128)(2,1)}, u32[]{:S(2)}, u32[]{:S(2)}) %collective-permute-start.17) | collective-permute-done | bytes 1179680 | tf_op jit(solution)/shard_map/ppermute | solution.py:95
  194.6 1.6 collective-permute-start.18
  198.9 7.5 %broadcast_select_fusion.2 = (bf16[512,512]{1,0:T(8,128)(2,1)}, bf16[512,512]{1,0:T(8,128)(2,1)S(1)}) fusion(bf16[512,512]{1,0:T(8,128)(2,1)} %fusion.26, pred[]{:T(512)S(6)} %eq.48, bf16[16,72,512]{2,1,0:T(8,128)(2,1)} %collective-permute-done.11, bf16[16,512,512]{2,1,0:T(8,128)(2,1)} %param.16, bf16[4,16,72,512]{3,2,1,0:T(8,128)(2,1)} %select_convert_fusion), kind=kOutput, calls=%fused_computation.78 | convolution fusion | flops 1209335808 | bytes 12320769 | tf_op jit(solution)/shard_map/ect,ecd->td/dot_general | solution.py:175
  206.3 7.1 %fusion.28 = bf16[512,512]{1,0:T(8,128)(2,1)} fusion(bf16[4,16,72,512]{3,2,1,0:T(8,128)(2,1)} %select_convert_fusion, bf16[16,72,512]{2,1,0:T(8,128)(2,1)} %collective-permute-done.17, bf16[16,512,512]{2,1,0:T(8,128)(2,1)} %param.16), kind=kOutput, calls=%fused_computation.47 | convolution fusion | flops 1208811520 | bytes 11272192 | tf_op jit(solution)/shard_map/ect,ecd->td/dot_general | solution.py:175
  213.5 4.8 %convolution_bitcast_fusion = f32[512,512]{1,0:T(8,128)} fusion(bf16[8,72,512]{2,1,0:T(8,128)(2,1)} %collective-permute-done.19, bf16[16,512,512]{2,1,0:T(8,128)(2,1)} %param.16, bf16[4,16,72,512]{3,2,1,0:T(8,128)(2,1)} %select_convert_fusion), kind=kOutput, calls=%fused_computation.35 | convolution fusion | flops 604274688 | bytes 6422528 | tf_op jit(solution)/shard_map/ect,ecd->td/dot_general | solution.py:175
  218.3 4.3 %broadcast_select_fusion = (bf16[512,512]{1,0:T(8,128)(2,1)S(1)}, bf16[512,512]{1,0:T(8,128)(2,1)S(1)}) fusion(bf16[512,512]{1,0:T(8,128)(2,1)} %fusion.28, pred[]{:T(512)S(6)} %eq.48, f32[512,512]{1,0:T(8,128)} %convolution_bitcast_fusion, bf16[8,72,512]{2,1,0:T(8,128)(2,1)} %collective-permute-done.18, bf16[16,512,512]{2,1,0:T(8,128)(2,1)} %param.16, ...), kind=kOutput, calls=%fused_computation.76 | convolution fusion | flops 605323264 | bytes 7995393 | tf_op jit(solution)/shard_map/ect,ecd->td/dot_general | solution.py:175
  224.5 2.0 collective-permute-start.15
  226.7 2.9 %collective-permute-start.21 = (bf16[128,512]{1,0:T(8,128)(2,1)S(1)}, bf16[128,512]{1,0:T(8,128)(2,1)S(1)}, u32[]{:S(2)}, u32[]{:S(2)}) collective-permute-start(bf16[128,512]{1,0:T(8,128)(2,1)S(1)} %get-tuple-element.22), channel_id=1, source_target_pairs={{0,6},{2,0},{4,2},{6,4},{1,7},{3,1},{5,3},{7,5},{8,14},{10,8},{12,... | collective-permute-start | bytes 393224 | tf_op jit(solution)/shard_map/ppermute | solution.py:98
  229.5 3.9 %collective-permute-done.13 = bf16[128,512]{1,0:T(8,128)(2,1)S(1)} collective-permute-done((bf16[128,512]{1,0:T(8,128)(2,1)S(1)}, bf16[128,512]{1,0:T(8,128)(2,1)S(1)}, u32[]{:S(2)}, u32[]{:S(2)}) %collective-permute-start.13) | collective-permute-done | bytes 131104 | tf_op jit(solution)/shard_map/ppermute | solution.py:98
  233.4 2.0 collective-permute-start.22
  235.5 9.1 %collective-permute-done.14 = bf16[128,512]{1,0:T(8,128)(2,1)S(1)} collective-permute-done((bf16[128,512]{1,0:T(8,128)(2,1)S(1)}, bf16[128,512]{1,0:T(8,128)(2,1)S(1)}, u32[]{:S(2)}, u32[]{:S(2)}) %collective-permute-start.14) | collective-permute-done | bytes 131104 | tf_op jit(solution)/shard_map/ppermute | solution.py:98
  245.3 4.2 %collective-permute-done.22 = bf16[128,512]{1,0:T(8,128)(2,1)S(1)} collective-permute-done((bf16[128,512]{1,0:T(8,128)(2,1)S(1)}, bf16[128,512]{1,0:T(8,128)(2,1)S(1)}, u32[]{:S(2)}, u32[]{:S(2)}) %collective-permute-start.22) | collective-permute-done | bytes 131104 | tf_op jit(solution)/shard_map/ppermute | solution.py:98
  250.2 5.6 %collective-permute-done.24 = bf16[128,512]{1,0:T(8,128)(2,1)S(1)} collective-permute-done((bf16[128,512]{1,0:T(8,128)(2,1)S(1)}, bf16[128,512]{1,0:T(8,128)(2,1)S(1)}, u32[]{:S(2)}, u32[]{:S(2)}) %collective-permute-start.24) | collective-permute-done | bytes 131104 | tf_op jit(solution)/shard_map/ppermute | solution.py:191
  (90 shorter events, 24.7 us)
Async XLA Ops:
  0.0 7.2 %copy-start = (bf16[2048,64]{0,1:T(8,128)(2,1)S(1)}, bf16[2048,64]{0,1:T(8,128)(2,1)}, u32[]{:S(2)}) copy-start(bf16[2048,64]{0,1:T(8,128)(2,1)} %param.13) | copy-start | bytes 786436
  0.0 7.2 %copy-start.5 = (s32[1,128,8]{1,2,0:T(8,128)S(1)}, s32[1,128,8]{1,2,0:T(8,128)}, u32[]{:S(2)}) copy-start(s32[1,128,8]{1,2,0:T(8,128)} %param.17) | copy-start | bytes 12292
  2.6 6.2 %collective-permute-start.2 = (bf16[64,512]{1,0:T(8,128)(2,1)S(1)}, bf16[64,512]{1,0:T(8,128)(2,1)S(1)}, u32[]{:S(2)}, u32[]{:S(2)}) collective-permute-start(bf16[64,512]{1,0:T(8,128)(2,1)S(1)} %get-tuple-element.26), channel_id=1, source_target_pairs={{0,24},{8,16},{16,8},{24,0},{1,25},{9,17},{17,9},{25,1},{2,26},{10... | collective-permute-start | bytes 196616 | tf_op jit(solution)/shard_map/ppermute | solution.py:95
  6.6 4.3 %collective-permute-start.1 = (bf16[64,512]{1,0:T(8,128)(2,1)S(1)}, bf16[64,512]{1,0:T(8,128)(2,1)S(1)}, u32[]{:S(2)}, u32[]{:S(2)}) collective-permute-start(bf16[64,512]{1,0:T(8,128)(2,1)S(1)} %get-tuple-element.27), channel_id=1, source_target_pairs={{0,16},{8,24},{16,0},{24,8},{1,17},{9,25},{17,1},{25,9},{2,18},{10... | collective-permute-start | bytes 196616 | tf_op jit(solution)/shard_map/ppermute | solution.py:95
  7.1 4.3 %collective-permute-start = (bf16[64,512]{1,0:T(8,128)(2,1)S(1)}, bf16[64,512]{1,0:T(8,128)(2,1)S(1)}, u32[]{:S(2)}, u32[]{:S(2)}) collective-permute-start(bf16[64,512]{1,0:T(8,128)(2,1)S(1)} %get-tuple-element.28), channel_id=1, source_target_pairs={{0,8},{8,0},{16,24},{24,16},{1,9},{9,1},{17,25},{25,17},{2,10},{10... | collective-permute-start | bytes 196616 | tf_op jit(solution)/shard_map/ppermute | solution.py:95
  11.4 54.4 %collective-permute-start.4 = (bf16[4,64,512]{2,1,0:T(8,128)(2,1)S(1)}, bf16[4,64,512]{2,1,0:T(8,128)(2,1)}, u32[]{:S(2)}, u32[]{:S(2)}) collective-permute-start(bf16[4,64,512]{2,1,0:T(8,128)(2,1)S(1)} %get-tuple-element.30), channel_id=1, source_target_pairs={{0,4},{2,6},{4,0},{6,2},{1,5},{3,7},{5,1},{7,3},{8,12},{10,14},{12... | collective-permute-start | bytes 786440 | tf_op jit(solution)/shard_map/ppermute | solution.py:101
  14.1 51.7 %collective-permute-start.3 = (bf16[4,64,512]{2,1,0:T(8,128)(2,1)S(1)}, bf16[4,64,512]{2,1,0:T(8,128)(2,1)S(1)}, u32[]{:S(2)}, u32[]{:S(2)}) collective-permute-start(bf16[4,64,512]{2,1,0:T(8,128)(2,1)S(1)} %get-tuple-element.30), channel_id=1, source_target_pairs={{0,2},{2,4},{4,6},{6,0},{1,3},{3,5},{5,7},{7,1},{8,10},{10,12},{12... | collective-permute-start | bytes 786440 | tf_op jit(solution)/shard_map/ppermute | solution.py:101
  15.6 50.2 %collective-permute-start.5 = (bf16[4,64,512]{2,1,0:T(8,128)(2,1)S(1)}, bf16[4,64,512]{2,1,0:T(8,128)(2,1)S(1)}, u32[]{:S(2)}, u32[]{:S(2)}) collective-permute-start(bf16[4,64,512]{2,1,0:T(8,128)(2,1)S(1)} %get-tuple-element.30), channel_id=1, source_target_pairs={{0,6},{2,0},{4,2},{6,4},{1,7},{3,1},{5,3},{7,5},{8,14},{10,8},{12,... | collective-permute-start | bytes 786440 | tf_op jit(solution)/shard_map/ppermute | solution.py:101
  67.9 2.9 %collective-permute-start.6 = (bf16[4,4,64,512]{3,2,1,0:T(8,128)(2,1)S(1)}, bf16[4,4,64,512]{3,2,1,0:T(8,128)(2,1)}, u32[]{:S(2)}, u32[]{:S(2)}) collective-permute-start(bf16[4,4,64,512]{3,2,1,0:T(8,128)(2,1)S(1)} %get-tuple-element.18), channel_id=1, source_target_pairs={{0,1},{1,0},{2,3},{3,2},{4,5},{5,4},{6,7},{7,6},{8,9},{9,8},{10,11... | collective-permute-start | bytes 3145736 | tf_op jit(solution)/shard_map/ppermute | solution.py:104
  70.7 5.4 %slice-start = ((s8[8388608]{0:T(1024)(128)(4,1)}), s8[4194304]{0:T(1024)(128)(4,1)S(1)}, s32[]{:S(2)}) async-start(s8[8388608]{0:T(1024)(128)(4,1)} %bitcast.124), calls=%async_computation | async-start | bytes 8388608
  72.7 3.4 %slice-start.1 = ((s8[8388608]{0:T(1024)(128)(4,1)}), s8[4194304]{0:T(1024)(128)(4,1)S(1)}, s32[]{:S(2)}) async-start(s8[8388608]{0:T(1024)(128)(4,1)} %bitcast.124), calls=%async_computation.1 | async-start | bytes 8388608
  75.7 4.8 %slice-start.2 = ((s8[8388608]{0:T(1024)(128)(4,1)}), s8[4194304]{0:T(1024)(128)(4,1)S(1)}, s32[]{:S(2)}) async-start(s8[8388608]{0:T(1024)(128)(4,1)} %bitcast.126), calls=%async_computation.2 | async-start | bytes 8388608
  76.1 4.4 %slice-start.3 = ((s8[8388608]{0:T(1024)(128)(4,1)}), s8[4194304]{0:T(1024)(128)(4,1)S(1)}, s32[]{:S(2)}) async-start(s8[8388608]{0:T(1024)(128)(4,1)} %bitcast.126), calls=%async_computation.3 | async-start | bytes 8388608
  79.0 53.5 %collective-permute-start.9 = (bf16[16,144,512]{2,1,0:T(8,128)(2,1)}, bf16[16,144,512]{2,1,0:T(8,128)(2,1)S(1)}, u32[]{:S(2)}, u32[]{:S(2)}) collective-permute-start(bf16[16,144,512]{2,1,0:T(8,128)(2,1)} %fusion.17), channel_id=1, source_target_pairs={{0,16},{8,24},{16,0},{24,8},{1,17},{9,25},{17,1},{25,9},{2,18},{10... | collective-permute-start | bytes 7077896 | tf_op jit(solution)/shard_map/ppermute | solution.py:95
  83.3 54.0 %collective-permute-start.7 = (bf16[16,144,512]{2,1,0:T(8,128)(2,1)}, bf16[16,144,512]{2,1,0:T(8,128)(2,1)S(1)}, u32[]{:S(2)}, u32[]{:S(2)}) collective-permute-start(bf16[16,144,512]{2,1,0:T(8,128)(2,1)} %fusion.18), channel_id=1, source_target_pairs={{0,8},{8,0},{16,24},{24,16},{1,9},{9,1},{17,25},{25,17},{2,10},{10... | collective-permute-start | bytes 7077896 | tf_op jit(solution)/shard_map/ppermute | solution.py:95
  137.2 27.2 %collective-permute-start.10 = (bf16[16,72,512]{2,1,0:T(8,128)(2,1)S(1)}, bf16[16,72,512]{2,1,0:T(8,128)(2,1)S(1)}, u32[]{:S(2)}, u32[]{:S(2)}) collective-permute-start(bf16[16,72,512]{2,1,0:T(8,128)(2,1)S(1)} %slice.187), channel_id=1, source_target_pairs={{0,8},{8,0},{16,24},{24,16},{1,9},{9,1},{17,25},{25,17},{2,10},{10... | collective-permute-start | bytes 3538952 | tf_op jit(solution)/shard_map/ppermute | solution.py:95
  138.9 27.2 %collective-permute-start.8 = (bf16[16,72,512]{2,1,0:T(8,128)(2,1)S(1)}, bf16[16,72,512]{2,1,0:T(8,128)(2,1)S(1)}, u32[]{:S(2)}, u32[]{:S(2)}) collective-permute-start(bf16[16,72,512]{2,1,0:T(8,128)(2,1)S(1)} %slice.188), channel_id=1, source_target_pairs={{0,16},{8,24},{16,0},{24,8},{1,17},{9,25},{17,1},{25,9},{2,18},{10... | collective-permute-start | bytes 3538952 | tf_op jit(solution)/shard_map/ppermute | solution.py:95
  167.1 26.4 %collective-permute-start.17 = (bf16[16,72,512]{2,1,0:T(8,128)(2,1)S(1)}, bf16[16,72,512]{2,1,0:T(8,128)(2,1)}, u32[]{:S(2)}, u32[]{:S(2)}) collective-permute-start(bf16[16,72,512]{2,1,0:T(8,128)(2,1)S(1)} %fusion.12), channel_id=1, source_target_pairs={{0,8},{8,0},{16,24},{24,16},{1,9},{9,1},{17,25},{25,17},{2,10},{10... | collective-permute-start | bytes 3538952 | tf_op jit(solution)/shard_map/ppermute | solution.py:95
  168.8 27.4 %collective-permute-start.11 = (bf16[16,72,512]{2,1,0:T(8,128)(2,1)S(1)}, bf16[16,72,512]{2,1,0:T(8,128)(2,1)}, u32[]{:S(2)}, u32[]{:S(2)}) collective-permute-start(bf16[16,72,512]{2,1,0:T(8,128)(2,1)S(1)} %fusion.12), channel_id=1, source_target_pairs={{0,16},{8,24},{16,0},{24,8},{1,17},{9,25},{17,1},{25,9},{2,18},{10... | collective-permute-start | bytes 3538952 | tf_op jit(solution)/shard_map/ppermute | solution.py:95
  194.6 23.7 %collective-permute-start.18 = (bf16[8,72,512]{2,1,0:T(8,128)(2,1)S(1)}, bf16[8,72,512]{2,1,0:T(8,128)(2,1)}, u32[]{:S(2)}, u32[]{:S(2)}) collective-permute-start(bf16[8,72,512]{2,1,0:T(8,128)(2,1)S(1)} %slice.132), channel_id=1, source_target_pairs={{0,16},{8,24},{16,0},{24,8},{1,17},{9,25},{17,1},{25,9},{2,18},{10... | collective-permute-start | bytes 1769480 | tf_op jit(solution)/shard_map/ppermute | solution.py:95
  197.3 16.1 %collective-permute-start.19 = (bf16[8,72,512]{2,1,0:T(8,128)(2,1)S(1)}, bf16[8,72,512]{2,1,0:T(8,128)(2,1)}, u32[]{:S(2)}, u32[]{:S(2)}) collective-permute-start(bf16[8,72,512]{2,1,0:T(8,128)(2,1)S(1)} %slice.134), channel_id=1, source_target_pairs={{0,8},{8,0},{16,24},{24,16},{1,9},{9,1},{17,25},{25,17},{2,10},{10... | collective-permute-start | bytes 1769480 | tf_op jit(solution)/shard_map/ppermute | solution.py:95
  206.3 16.9 %collective-permute-start.12 = (bf16[4,128,512]{2,1,0:T(8,128)(2,1)}, bf16[4,128,512]{2,1,0:T(8,128)(2,1)}, u32[]{:S(2)}, u32[]{:S(2)}) collective-permute-start(bf16[4,128,512]{2,1,0:T(8,128)(2,1)} %bitcast.138), channel_id=1, source_target_pairs={{0,1},{1,0},{2,3},{3,2},{4,5},{5,4},{6,7},{7,6},{8,9},{9,8},{10,11... | collective-permute-start | bytes 1572872 | tf_op jit(solution)/shard_map/ppermute | solution.py:104
  222.6 3.9 %collective-permute-start.20 = (bf16[4,128,512]{2,1,0:T(8,128)(2,1)S(1)}, bf16[4,128,512]{2,1,0:T(8,128)(2,1)S(1)}, u32[]{:S(2)}, u32[]{:S(2)}) collective-permute-start(bf16[4,128,512]{2,1,0:T(8,128)(2,1)S(1)} %bitcast.137), channel_id=1, source_target_pairs={{0,1},{1,0},{2,3},{3,2},{4,5},{5,4},{6,7},{7,6},{8,9},{9,8},{10,11... | collective-permute-start | bytes 1572872 | tf_op jit(solution)/shard_map/ppermute | solution.py:104
  224.4 9.0 %collective-permute-start.13 = (bf16[128,512]{1,0:T(8,128)(2,1)S(1)}, bf16[128,512]{1,0:T(8,128)(2,1)S(1)}, u32[]{:S(2)}, u32[]{:S(2)}) collective-permute-start(bf16[128,512]{1,0:T(8,128)(2,1)S(1)} %get-tuple-element.19), channel_id=1, source_target_pairs={{0,6},{2,0},{4,2},{6,4},{1,7},{3,1},{5,3},{7,5},{8,14},{10,8},{12,... | collective-permute-start | bytes 393224 | tf_op jit(solution)/shard_map/ppermute | solution.py:98
  224.5 11.0 %collective-permute-start.15 = (bf16[128,512]{1,0:T(8,128)(2,1)S(1)}, bf16[128,512]{1,0:T(8,128)(2,1)S(1)}, u32[]{:S(2)}, u32[]{:S(2)}) collective-permute-start(bf16[128,512]{1,0:T(8,128)(2,1)S(1)} %get-tuple-element.20), channel_id=1, source_target_pairs={{0,2},{2,4},{4,6},{6,0},{1,3},{3,5},{5,7},{7,1},{8,10},{10,12},{12... | collective-permute-start | bytes 393224 | tf_op jit(solution)/shard_map/ppermute | solution.py:98
  226.5 18.0 %collective-permute-start.14 = (bf16[128,512]{1,0:T(8,128)(2,1)S(1)}, bf16[128,512]{1,0:T(8,128)(2,1)S(1)}, u32[]{:S(2)}, u32[]{:S(2)}) collective-permute-start(bf16[128,512]{1,0:T(8,128)(2,1)S(1)} %get-tuple-element.21), channel_id=1, source_target_pairs={{0,4},{2,6},{4,0},{6,2},{1,5},{3,7},{5,1},{7,3},{8,12},{10,14},{12... | collective-permute-start | bytes 393224 | tf_op jit(solution)/shard_map/ppermute | solution.py:98
  226.5 30.1 %copy-start.1 = (bf16[2048,64]{0,1:T(8,128)(2,1)S(1)}, bf16[2048,64]{0,1:T(8,128)(2,1)}, u32[]{:S(2)}) copy-start(bf16[2048,64]{0,1:T(8,128)(2,1)} %param.13) | copy-start | bytes 786436
  226.7 18.6 %collective-permute-start.21 = (bf16[128,512]{1,0:T(8,128)(2,1)S(1)}, bf16[128,512]{1,0:T(8,128)(2,1)S(1)}, u32[]{:S(2)}, u32[]{:S(2)}) collective-permute-start(bf16[128,512]{1,0:T(8,128)(2,1)S(1)} %get-tuple-element.22), channel_id=1, source_target_pairs={{0,6},{2,0},{4,2},{6,4},{1,7},{3,1},{5,3},{7,5},{8,14},{10,8},{12,... | collective-permute-start | bytes 393224 | tf_op jit(solution)/shard_map/ppermute | solution.py:98
  229.5 15.8 %collective-permute-start.23 = (bf16[128,512]{1,0:T(8,128)(2,1)S(1)}, bf16[128,512]{1,0:T(8,128)(2,1)S(1)}, u32[]{:S(2)}, u32[]{:S(2)}) collective-permute-start(bf16[128,512]{1,0:T(8,128)(2,1)S(1)} %get-tuple-element.23), channel_id=1, source_target_pairs={{0,2},{2,4},{4,6},{6,0},{1,3},{3,5},{5,7},{7,1},{8,10},{10,12},{12... | collective-permute-start | bytes 393224 | tf_op jit(solution)/shard_map/ppermute | solution.py:98
  233.4 16.1 %collective-permute-start.22 = (bf16[128,512]{1,0:T(8,128)(2,1)S(1)}, bf16[128,512]{1,0:T(8,128)(2,1)S(1)}, u32[]{:S(2)}, u32[]{:S(2)}) collective-permute-start(bf16[128,512]{1,0:T(8,128)(2,1)S(1)} %get-tuple-element.24), channel_id=1, source_target_pairs={{0,4},{2,6},{4,0},{6,2},{1,5},{3,7},{5,1},{7,3},{8,12},{10,14},{12... | collective-permute-start | bytes 393224 | tf_op jit(solution)/shard_map/ppermute | solution.py:98
  244.6 5.6 %collective-permute-start.16 = (bf16[128,512]{1,0:T(8,128)(2,1)S(1)}, bf16[128,512]{1,0:T(8,128)(2,1)S(1)}, u32[]{:S(2)}, u32[]{:S(2)}) collective-permute-start(bf16[128,512]{1,0:T(8,128)(2,1)S(1)} %fusion.48), channel_id=1, source_target_pairs={{0,0},{1,16},{8,8},{9,24},{16,17},{17,1},{24,25},{25,9},{2,2},{3,1... | collective-permute-start | bytes 393224 | tf_op jit(solution)/shard_map/ppermute | solution.py:191
  249.6 6.3 %collective-permute-start.24 = (bf16[128,512]{1,0:T(8,128)(2,1)S(1)}, bf16[128,512]{1,0:T(8,128)(2,1)S(1)}, u32[]{:S(2)}, u32[]{:S(2)}) collective-permute-start(bf16[128,512]{1,0:T(8,128)(2,1)S(1)} %fusion.45), channel_id=1, source_target_pairs={{0,8},{1,24},{8,0},{9,16},{16,25},{17,9},{24,17},{25,1},{2,10},{3,... | collective-permute-start | bytes 393224 | tf_op jit(solution)/shard_map/ppermute | solution.py:191
  (3 other events, 2.9 us)

commit v3 on v2

--- a/solution.py
+++ b/solution.py
@@ -124,14 +124,10 @@
     onehot_k = (routes[0][:, :, None] == jnp.arange(experts_all, dtype=jnp.int32)).astype(jnp.float32)
     picked = jnp.sum(onehot_k * prob[:, None, :], axis=-1)
     gates = picked / jnp.sum(picked, axis=1, keepdims=True)
-    table = jnp.concatenate([routes[0].astype(jnp.float32), gates], axis=1)
-    table = lax.all_gather(table, ("section", "expert"), axis=0, tiled=False)
-    table = table.reshape(sections, zs, tok_count, 2 * TOPK)
-    table = jnp.stack([lax.dynamic_index_in_dim(table, me ^ j, 0, False) for j in range(sections)])
-    table = jnp.stack(
-        [lax.dynamic_index_in_dim(table, lax.rem(z + zs - k, zs), 1, False) for k in range(zs)], axis=1
-    )
-    table = table.reshape(sections, sec_toks, 2 * TOPK)
+    table = jnp.concatenate([routes[0].astype(jnp.float32), gates], axis=1).T
+    table = jnp.stack([table if j == 0 else to_section(table, j) for j in range(sections)])
+    table = jnp.stack([table if k == 0 else to_upper(table, k) for k in range(zs)], axis=1)
+    table = table.transpose(0, 1, 3, 2).reshape(sections, sec_toks, 2 * TOPK)
     all_routes, all_gates = table[..., :TOPK].astype(jnp.int32), table[..., TOPK:]
 
     own = z * local_count + jnp.arange(local_count, dtype=jnp.int32)
@@ -152,21 +148,15 @@
         "sect,std->secd", dispatch, rows, preferred_element_type=jnp.float32
     ).astype(jnp.bfloat16)
 
-    def product(a, b, weight):
-        x = jnp.concatenate([grouped[a], grouped[b]], axis=1)
-        return jnp.einsum("ecd,edh->ech", x, weight, preferred_element_type=jnp.float32)
-
-    def summed(weight, near, far):
-        got = to_section(product(near, 3, weight).astype(jnp.bfloat16), near)
-        both = product(0, far, weight) + got.astype(jnp.float32)
+    def product(a, b, weight, lo, hi):
+        x = jnp.concatenate([grouped[a, lo:hi], grouped[b, lo:hi]], axis=1)
+        return jnp.einsum("ecd,edh->ech", x, weight[lo:hi], preferred_element_type=jnp.float32)
+
+    def summed(weight, near, far, lo, hi):
+        got = to_section(product(near, 3, weight, lo, hi).astype(jnp.bfloat16), near)
+        both = product(0, far, weight, lo, hi) + got.astype(jnp.float32)
         got = to_section(both[:, slots:].astype(jnp.bfloat16), far)
         return both[:, :slots] + got.astype(jnp.float32)
-
-    act = (jax.nn.silu(summed(gate_w, 1, 2)) * summed(up_w, 2, 1)).astype(jnp.bfloat16)
-
-    act1, act2 = to_section(act, 1), to_section(act, 2)
-    cut = local_count // 2
-    act3 = (to_section(act1[:cut], 2), to_section(act2[cut:], 1))
 
     def gated_sum(j, a, lo, hi):
         out = jnp.einsum(
@@ -175,6 +165,17 @@
         return jnp.einsum(
             "ect,ecd->td", combine[j, lo:hi], out, preferred_element_type=jnp.float32
         )
+
+    halfway = local_count // 2
+    acts = []
+    for lo, hi in ((0, halfway), (halfway, local_count)):
+        gate, up = summed(gate_w, 1, 2, lo, hi), summed(up_w, 2, 1, lo, hi)
+        act = (jax.nn.silu(gate) * up).astype(jnp.bfloat16)
+        act1, act2 = to_section(act, 1), to_section(act, 2)
+        cut = (hi - lo) // 2
+        act3 = jnp.concatenate([to_section(act1[:cut], 2), to_section(act2[cut:], 1)], axis=0)
+        acts.append((act, act1, act2, act3))
+    blocks = [jnp.concatenate([part[j] for part in acts], axis=0) for j in range(sections)]
 
     def deliver(low, high, shift):
         low, high = (b.astype(jnp.bfloat16).reshape(zs, tok_count, depth) for b in (low, high))
@@ -190,11 +191,8 @@
                 moves.append((s * pairs + p, (s ^ (shift + 2 * p)) * pairs + s // 2))
         return lax.ppermute(total.astype(jnp.bfloat16), ("section", "pair"), moves)
 
-    block0 = gated_sum(0, act, 0, local_count)
-    block1 = gated_sum(1, act1, 0, local_count)
-    block2 = gated_sum(2, act2, 0, local_count)
+    block0, block1, block2, block3 = (gated_sum(j, blocks[j], 0, local_count) for j in range(sections))
     same = deliver(block0, block2, 0)
-    block3 = gated_sum(3, act3[0], 0, cut) + gated_sum(3, act3[1], cut, local_count)
     unlike = deliver(block1, block3, 1)
     moe = jnp.where(
         me % 2 == 0,

time: 257 us -> 224 us (0.87)
  blocking collectives: 47.7 us -> 0 us
  starting transfers between devices: 29.7 us -> 45 us
  matrix products: 44.3 us -> 37.7 us
  waiting for transfers between devices: 114 us -> 120 us
    all_gather x1 -> x0, blocking collectives: 47.7 us -> none  [move_tokens(): table = lax.all_gather(table, ('section', 'expert'), axis=0, tiled=False)]
    ppermute x3 -> x6, waiting for transfers between devices: 0.01 us -> 15.6 us  [to_upper(): return lax.ppermute(x, 'expert', [(i, (i + k) % zs) for i in range(zs)])]
    ppermute x3 -> x6, starting transfers between devices: 6.48 us -> 14.3 us  [to_upper(): return lax.ppermute(x, 'expert', [(i, (i + k) % zs) for i in range(zs)])]
    ppermute x11 -> x22, waiting for transfers between devices: 89.3 us -> 81.8 us  [to_section(): return lax.ppermute(x, 'section', [(s, s ^ j) for s in range(sections)])]
    ppermute x11 -> x22, starting transfers between devices: 14.3 us -> 21 us  [to_section(): return lax.ppermute(x, 'section', [(s, s ^ j) for s in range(sections)])]
    dot_general x4 -> x8, matrix products: 10.2 us -> 6.3 us  [product(): jnp.einsum('ecd,edh->ech', x, weight[lo:hi], preferred_element_type=jnp.f...]
    dot_general x5 -> x4, matrix products: 30.6 us -> 27.9 us  [gated_sum(): jnp.einsum('ect,ecd->td', combine[j, lo:hi], out, preferred_element_type=...]
  transfers between devices with their start and end apart: 25 -> 39, of which waited for: 12 -> 21; matrix products, arithmetic and copies ran while one was open for 19% -> 21% of each run, Pallas kernels for 0% -> 0%
where the time goes in v3:
time: 224 us; the launch traced here: 223 us
  waiting for transfers between devices  120 us (54%)
  starting transfers between devices  45 us (20%)
  matrix products  37.7 us (17%)
  other arithmetic  13.8 us (6%)
  local copies, waits for them, and re-layouts  6.59 us (3%)
    ppermute x22, waiting for transfers between devices, to_section(): return lax.ppermute(x, 'section', [(s, s ^ j) for s in range(sections)])  81.8 us
    dot_general x4, matrix products, gated_sum(): jnp.einsum('ect,ecd->td', combine[j, lo:hi], out, preferred_element_type=...  27.9 us
    ppermute x22, starting transfers between devices, to_section(): return lax.ppermute(x, 'section', [(s, s ^ j) for s in range(sections)])  21 us
    ppermute x6, waiting for transfers between devices, to_lower(): return lax.ppermute(x, 'expert', [(i, (i - k) % zs) for i in range(zs)])  17.5 us
    ppermute x6, waiting for transfers between devices, to_upper(): return lax.ppermute(x, 'expert', [(i, (i + k) % zs) for i in range(zs)])  15.6 us
    ppermute x6, starting transfers between devices, to_upper(): return lax.ppermute(x, 'expert', [(i, (i + k) % zs) for i in range(zs)])  14.3 us
    ppermute x6, starting transfers between devices, to_lower(): return lax.ppermute(x, 'expert', [(i, (i - k) % zs) for i in range(zs)])  7.71 us
    dot_general x8, matrix products, product(): jnp.einsum('ecd,edh->ech', x, weight[lo:hi], preferred_element_type=jnp.f...  6.3 us
  transfers between devices with their start and end apart: 39, of which 21 were waited for; matrix products, arithmetic and copies ran while one was open for 21% of the time, Pallas kernels for 0%

profile of v3, /device:TPU:0, one launch (start us, length us, event | category | flops | bytes accessed | tf_op | source)
XLA Modules:
  0.0 223.3 jit_solution(9528485840374408392)
XLA Ops:
  0.0 1.6 multiply_reduce_fusion
  2.6 3.0 %collective-permute-start.6 = (bf16[64,512]{1,0:T(8,128)(2,1)S(1)}, bf16[64,512]{1,0:T(8,128)(2,1)S(1)}, u32[]{:S(2)}, u32[]{:S(2)}) collective-permute-start(bf16[64,512]{1,0:T(8,128)(2,1)S(1)} %get-tuple-element.32), channel_id=1, source_target_pairs={{0,8},{8,0},{16,24},{24,16},{1,9},{9,1},{17,25},{25,17},{2,10},{10... | collective-permute-start | bytes 196616 | tf_op jit(solution)/shard_map/ppermute | solution.py:95
  5.6 1.5 collective-permute-start.7
  8.0 1.9 collective-permute-done.7
  9.9 2.4 %collective-permute-done.8 = bf16[64,512]{1,0:T(8,128)(2,1)S(1)} collective-permute-done((bf16[64,512]{1,0:T(8,128)(2,1)S(1)}, bf16[64,512]{1,0:T(8,128)(2,1)S(1)}, u32[]{:S(2)}, u32[]{:S(2)}) %collective-permute-start.8) | collective-permute-done | bytes 65568 | tf_op jit(solution)/shard_map/ppermute | solution.py:95
  12.4 1.6 collective-permute-start.9
  14.0 2.6 %collective-permute-start.10 = (bf16[4,64,512]{2,1,0:T(8,128)(2,1)S(1)}, bf16[4,64,512]{2,1,0:T(8,128)(2,1)S(1)}, u32[]{:S(2)}, u32[]{:S(2)}) collective-permute-start(bf16[4,64,512]{2,1,0:T(8,128)(2,1)S(1)} %get-tuple-element.34), channel_id=1, source_target_pairs={{0,4},{2,6},{4,0},{6,2},{1,5},{3,7},{5,1},{7,3},{8,12},{10,14},{12... | collective-permute-start | bytes 786440 | tf_op jit(solution)/shard_map/ppermute | solution.py:101
  19.0 4.5 %collective-permute-done.9 = bf16[4,64,512]{2,1,0:T(8,128)(2,1)S(1)} collective-permute-done((bf16[4,64,512]{2,1,0:T(8,128)(2,1)S(1)}, bf16[4,64,512]{2,1,0:T(8,128)(2,1)S(1)}, u32[]{:S(2)}, u32[]{:S(2)}) %collective-permute-start.9) | collective-permute-done | bytes 262176 | tf_op jit(solution)/shard_map/ppermute | solution.py:101
  23.8 8.1 %collective-permute-done.10 = bf16[4,64,512]{2,1,0:T(8,128)(2,1)S(1)} collective-permute-done((bf16[4,64,512]{2,1,0:T(8,128)(2,1)S(1)}, bf16[4,64,512]{2,1,0:T(8,128)(2,1)S(1)}, u32[]{:S(2)}, u32[]{:S(2)}) %collective-permute-start.10) | collective-permute-done | bytes 262176 | tf_op jit(solution)/shard_map/ppermute | solution.py:101
  34.1 6.1 %collective-permute-start.3 = (f32[4,16,128]{2,1,0:T(8,128)S(1)}, f32[4,16,128]{2,1,0:T(8,128)S(1)}, u32[]{:S(2)}, u32[]{:S(2)}) collective-permute-start(f32[4,16,128]{2,1,0:T(8,128)S(1)} %get-tuple-element.38), channel_id=1, source_target_pairs={{0,2},{2,4},{4,6},{6,0},{1,3},{3,5},{5,7},{7,1},{8,10},{10,12},{12... | collective-permute-start | bytes 98312 | tf_op jit(solution)/shard_map/ppermute | solution.py:101
  40.2 1.7 collective-permute-start.4
  43.4 2.1 collective-permute-done.4
  46.9 1.9 maximum_select_fusion
  48.8 3.0 %fusion.18 = bf16[4,16,72,512]{3,2,1,0:T(8,128)(2,1)S(1)} fusion(bf16[4,512,512,1]{2,1,3,0:T(8,128)(2,1)S(1)} %bitcast.132, s32[4,16,512]{2,1,0:T(8,128)S(1)} %fusion.71), kind=kOutput, calls=%fused_computation.20 | convolution fusion | flops 2420637696 | bytes 6946816 | tf_op jit(solution)/shard_map/sect,std->secd/dot_general | solution.py:147
  58.2 1.5 collective-permute-start.19
  59.8 22.3 %collective-permute-done.13 = bf16[8,144,512]{2,1,0:T(8,128)(2,1)S(1)} collective-permute-done((bf16[8,144,512]{2,1,0:T(8,128)(2,1)S(1)}, bf16[8,144,512]{2,1,0:T(8,128)(2,1)S(1)}, u32[]{:S(2)}, u32[]{:S(2)}) %collective-permute-start.13) | collective-permute-done | bytes 1179680 | tf_op jit(solution)/shard_map/ppermute | solution.py:95
  85.9 21.5 %collective-permute-done.17 = bf16[8,144,512]{2,1,0:T(8,128)(2,1)S(1)} collective-permute-done((bf16[8,144,512]{2,1,0:T(8,128)(2,1)S(1)}, bf16[8,144,512]{2,1,0:T(8,128)(2,1)S(1)}, u32[]{:S(2)}, u32[]{:S(2)}) %collective-permute-start.17) | collective-permute-done | bytes 1179680 | tf_op jit(solution)/shard_map/ppermute | solution.py:95
  111.2 5.1 %select_convert_fusion = bf16[4,16,72,512]{3,2,1,0:T(8,128)(2,1)} fusion(bf16[4,16,512]{2,1,0:T(8,128)(2,1)S(1)} %fusion.75, s32[4,16,512]{2,1,0:T(8,128)S(1)} %fusion.71), kind=kLoop, calls=%fused_computation | loop fusion | flops 4718592 | bytes 4915200 | tf_op jit(solution)/shard_map/convert_element_type | solution.py:145
  116.3 5.6 %collective-permute-done.14 = bf16[8,72,512]{2,1,0:T(8,128)(2,1)S(1)} collective-permute-done((bf16[8,72,512]{2,1,0:T(8,128)(2,1)S(1)}, bf16[8,72,512]{2,1,0:T(8,128)(2,1)S(1)}, u32[]{:S(2)}, u32[]{:S(2)}) %collective-permute-start.14) | collective-permute-done | bytes 589856 | tf_op jit(solution)/shard_map/ppermute | solution.py:95
  123.9 10.6 %collective-permute-done.18 = bf16[8,72,512]{2,1,0:T(8,128)(2,1)S(1)} collective-permute-done((bf16[8,72,512]{2,1,0:T(8,128)(2,1)S(1)}, bf16[8,72,512]{2,1,0:T(8,128)(2,1)S(1)}, u32[]{:S(2)}, u32[]{:S(2)}) %collective-permute-start.18) | collective-permute-done | bytes 589856 | tf_op jit(solution)/shard_map/ppermute | solution.py:95
  136.6 7.1 %fusion.31 = bf16[512,512]{1,0:T(8,128)(2,1)} fusion(bf16[4,16,72,512]{3,2,1,0:T(8,128)(2,1)} %select_convert_fusion, bf16[16,512,512]{2,1,0:T(8,128)(2,1)} %param.16, bf16[8,72,512]{2,1,0:T(8,128)(2,1)S(1)} %fusion.44, bf16[8,72,512]{2,1,0:T(8,128)(2,1)S(1)} %fusion.46), kind=kOutput, calls=%fused_computation.48 | convolution fusion | flops 1209401344 | bytes 11272192 | tf_op jit(solution)/shard_map/ect,ecd->td/dot_general | solution.py:165
  143.6 3.5 %collective-permute-done.21 = bf16[8,72,512]{2,1,0:T(8,128)(2,1)S(1)} collective-permute-done((bf16[8,72,512]{2,1,0:T(8,128)(2,1)S(1)}, bf16[8,72,512]{2,1,0:T(8,128)(2,1)S(1)}, u32[]{:S(2)}, u32[]{:S(2)}) %collective-permute-start.21) | collective-permute-done | bytes 589856 | tf_op jit(solution)/shard_map/ppermute | solution.py:95
  147.9 10.1 %collective-permute-done.22 = bf16[8,72,512]{2,1,0:T(8,128)(2,1)} collective-permute-done((bf16[8,72,512]{2,1,0:T(8,128)(2,1)S(1)}, bf16[8,72,512]{2,1,0:T(8,128)(2,1)}, u32[]{:S(2)}, u32[]{:S(2)}) %collective-permute-start.22) | collective-permute-done | bytes 589856 | tf_op jit(solution)/shard_map/ppermute | solution.py:95
  158.1 7.2 %broadcast_select_fusion.2 = (bf16[512,512]{1,0:T(8,128)(2,1)}, bf16[512,512]{1,0:T(8,128)(2,1)S(1)}) fusion(bf16[512,512]{1,0:T(8,128)(2,1)} %fusion.31, pred[]{:T(512)S(6)} %eq.48, bf16[16,512,512]{2,1,0:T(8,128)(2,1)} %param.16, bf16[8,72,512]{2,1,0:T(8,128)(2,1)} %collective-permute-done.22, bf16[8,72,512]{2,1,0:T(8,128)(2,1)} %copy-done.5, ...), kind=kOutput, calls=%fused_computation.120 | convolution fusion | flops 1209925632 | bytes 12320769 | tf_op jit(solution)/shard_map/ect,ecd->td/dot_general | solution.py:165
  170.3 1.5 collective-permute-start.32
  173.6 7.2 %fusion.33 = bf16[512,512]{1,0:T(8,128)(2,1)} fusion(bf16[4,16,72,512]{3,2,1,0:T(8,128)(2,1)} %select_convert_fusion, bf16[16,512,512]{2,1,0:T(8,128)(2,1)} %param.16, bf16[8,72,512]{2,1,0:T(8,128)(2,1)} %collective-permute-done.29, bf16[8,72,512]{2,1,0:T(8,128)(2,1)} %collective-permute-done.28), kind=kOutput, calls=%fused_computation.50 | convolution fusion | flops 1209401344 | bytes 11272192 | tf_op jit(solution)/shard_map/ect,ecd->td/dot_general | solution.py:165
  183.5 6.4 %broadcast_select_fusion = (bf16[512,512]{1,0:T(8,128)(2,1)S(1)}, bf16[512,512]{1,0:T(8,128)(2,1)S(1)}) fusion(bf16[512,512]{1,0:T(8,128)(2,1)} %fusion.33, pred[]{:T(512)S(6)} %eq.48, bf16[16,512,512]{2,1,0:T(8,128)(2,1)} %param.16, bf16[4,72,512]{2,1,0:T(8,128)(2,1)} %collective-permute-done.33, bf16[4,72,512]{2,1,0:T(8,128)(2,1)} %collective-permute-done.32, ...), kind=kOutput, calls=%fused_computation.118 | convolution fusion | flops 1211105280 | bytes 12320769 | tf_op jit(solution)/shard_map/ect,ecd->td/dot_general | solution.py:165
  190.2 2.7 %collective-permute-start.24 = (bf16[128,512]{1,0:T(8,128)(2,1)S(1)}, bf16[128,512]{1,0:T(8,128)(2,1)S(1)}, u32[]{:S(2)}, u32[]{:S(2)}) collective-permute-start(bf16[128,512]{1,0:T(8,128)(2,1)S(1)} %get-tuple-element.23), channel_id=1, source_target_pairs={{0,6},{2,0},{4,2},{6,4},{1,7},{3,1},{5,3},{7,5},{8,14},{10,8},{12,... | collective-permute-start | bytes 393224 | tf_op jit(solution)/shard_map/ppermute | solution.py:98
  193.7 3.2 %collective-permute-start.35 = (bf16[128,512]{1,0:T(8,128)(2,1)S(1)}, bf16[128,512]{1,0:T(8,128)(2,1)S(1)}, u32[]{:S(2)}, u32[]{:S(2)}) collective-permute-start(bf16[128,512]{1,0:T(8,128)(2,1)S(1)} %get-tuple-element.26), channel_id=1, source_target_pairs={{0,6},{2,0},{4,2},{6,4},{1,7},{3,1},{5,3},{7,5},{8,14},{10,8},{12,... | collective-permute-start | bytes 393224 | tf_op jit(solution)/shard_map/ppermute | solution.py:98
  198.1 7.7 %collective-permute-done.25 = bf16[128,512]{1,0:T(8,128)(2,1)S(1)} collective-permute-done((bf16[128,512]{1,0:T(8,128)(2,1)S(1)}, bf16[128,512]{1,0:T(8,128)(2,1)S(1)}, u32[]{:S(2)}, u32[]{:S(2)}) %collective-permute-start.25) | collective-permute-done | bytes 131104 | tf_op jit(solution)/shard_map/ppermute | solution.py:98
  206.6 9.8 %collective-permute-done.36 = bf16[128,512]{1,0:T(8,128)(2,1)S(1)} collective-permute-done((bf16[128,512]{1,0:T(8,128)(2,1)S(1)}, bf16[128,512]{1,0:T(8,128)(2,1)S(1)}, u32[]{:S(2)}, u32[]{:S(2)}) %collective-permute-start.36) | collective-permute-done | bytes 131104 | tf_op jit(solution)/shard_map/ppermute | solution.py:98
  217.6 4.9 %collective-permute-done.38 = bf16[128,512]{1,0:T(8,128)(2,1)S(1)} collective-permute-done((bf16[128,512]{1,0:T(8,128)(2,1)S(1)}, bf16[128,512]{1,0:T(8,128)(2,1)S(1)}, u32[]{:S(2)}, u32[]{:S(2)}) %collective-permute-start.38) | collective-permute-done | bytes 131104 | tf_op jit(solution)/shard_map/ppermute | solution.py:192
  (121 shorter events, 43.0 us)
Async XLA Ops:
  12.4 11.2 %collective-permute-start.9 = (bf16[4,64,512]{2,1,0:T(8,128)(2,1)S(1)}, bf16[4,64,512]{2,1,0:T(8,128)(2,1)S(1)}, u32[]{:S(2)}, u32[]{:S(2)}) collective-permute-start(bf16[4,64,512]{2,1,0:T(8,128)(2,1)S(1)} %get-tuple-element.34), channel_id=1, source_target_pairs={{0,2},{2,4},{4,6},{6,0},{1,3},{3,5},{5,7},{7,1},{8,10},{10,12},{12... | collective-permute-start | bytes 786440 | tf_op jit(solution)/shard_map/ppermute | solution.py:101
  14.0 17.9 %collective-permute-start.10 = (bf16[4,64,512]{2,1,0:T(8,128)(2,1)S(1)}, bf16[4,64,512]{2,1,0:T(8,128)(2,1)S(1)}, u32[]{:S(2)}, u32[]{:S(2)}) collective-permute-start(bf16[4,64,512]{2,1,0:T(8,128)(2,1)S(1)} %get-tuple-element.34), channel_id=1, source_target_pairs={{0,4},{2,6},{4,0},{6,2},{1,5},{3,7},{5,1},{7,3},{8,12},{10,14},{12... | collective-permute-start | bytes 786440 | tf_op jit(solution)/shard_map/ppermute | solution.py:101
  16.6 15.4 %collective-permute-start.11 = (bf16[4,64,512]{2,1,0:T(8,128)(2,1)S(1)}, bf16[4,64,512]{2,1,0:T(8,128)(2,1)S(1)}, u32[]{:S(2)}, u32[]{:S(2)}) collective-permute-start(bf16[4,64,512]{2,1,0:T(8,128)(2,1)S(1)} %get-tuple-element.34), channel_id=1, source_target_pairs={{0,6},{2,0},{4,2},{6,4},{1,7},{3,1},{5,3},{7,5},{8,14},{10,8},{12,... | collective-permute-start | bytes 786440 | tf_op jit(solution)/shard_map/ppermute | solution.py:101
  17.9 16.1 %collective-permute-start = (f32[16,128]{1,0:T(8,128)S(1)}, f32[16,128]{1,0:T(8,128)S(1)}, u32[]{:S(2)}, u32[]{:S(2)}) collective-permute-start(f32[16,128]{1,0:T(8,128)S(1)} %get-tuple-element.40), channel_id=1, source_target_pairs={{0,8},{8,0},{16,24},{24,16},{1,9},{9,1},{17,25},{25,17},{2,10},{10... | collective-permute-start | bytes 24584 | tf_op jit(solution)/shard_map/ppermute | solution.py:95
  18.5 15.6 %collective-permute-start.1 = (f32[16,128]{1,0:T(8,128)S(1)}, f32[16,128]{1,0:T(8,128)S(1)}, u32[]{:S(2)}, u32[]{:S(2)}) collective-permute-start(f32[16,128]{1,0:T(8,128)S(1)} %get-tuple-element.40), channel_id=1, source_target_pairs={{0,16},{8,24},{16,0},{24,8},{1,17},{9,25},{17,1},{25,9},{2,18},{10... | collective-permute-start | bytes 24584 | tf_op jit(solution)/shard_map/ppermute | solution.py:95
  23.5 10.6 %collective-permute-start.2 = (f32[16,128]{1,0:T(8,128)S(1)}, f32[16,128]{1,0:T(8,128)S(1)}, u32[]{:S(2)}, u32[]{:S(2)}) collective-permute-start(f32[16,128]{1,0:T(8,128)S(1)} %get-tuple-element.40), channel_id=1, source_target_pairs={{0,24},{8,16},{16,8},{24,0},{1,25},{9,17},{17,9},{25,1},{2,26},{10... | collective-permute-start | bytes 24584 | tf_op jit(solution)/shard_map/ppermute | solution.py:95
  34.0 12.8 %collective-permute-start.12 = (bf16[4,4,64,512]{3,2,1,0:T(8,128)(2,1)S(1)}, bf16[4,4,64,512]{3,2,1,0:T(8,128)(2,1)}, u32[]{:S(2)}, u32[]{:S(2)}) collective-permute-start(bf16[4,4,64,512]{3,2,1,0:T(8,128)(2,1)S(1)} %get-tuple-element.22), channel_id=1, source_target_pairs={{0,1},{1,0},{2,3},{3,2},{4,5},{5,4},{6,7},{7,6},{8,9},{9,8},{10,11... | collective-permute-start | bytes 3145736 | tf_op jit(solution)/shard_map/ppermute | solution.py:104
  34.1 9.2 %collective-permute-start.3 = (f32[4,16,128]{2,1,0:T(8,128)S(1)}, f32[4,16,128]{2,1,0:T(8,128)S(1)}, u32[]{:S(2)}, u32[]{:S(2)}) collective-permute-start(f32[4,16,128]{2,1,0:T(8,128)S(1)} %get-tuple-element.38), channel_id=1, source_target_pairs={{0,2},{2,4},{4,6},{6,0},{1,3},{3,5},{5,7},{7,1},{8,10},{10,12},{12... | collective-permute-start | bytes 98312 | tf_op jit(solution)/shard_map/ppermute | solution.py:101
  53.1 29.0 %collective-permute-start.13 = (bf16[8,144,512]{2,1,0:T(8,128)(2,1)S(1)}, bf16[8,144,512]{2,1,0:T(8,128)(2,1)S(1)}, u32[]{:S(2)}, u32[]{:S(2)}) collective-permute-start(bf16[8,144,512]{2,1,0:T(8,128)(2,1)S(1)} %fusion.19), channel_id=1, source_target_pairs={{0,8},{8,0},{16,24},{24,16},{1,9},{9,1},{17,25},{25,17},{2,10},{10... | collective-permute-start | bytes 3538952 | tf_op jit(solution)/shard_map/ppermute | solution.py:95
  55.0 29.0 %collective-permute-start.15 = (bf16[8,144,512]{2,1,0:T(8,128)(2,1)S(1)}, bf16[8,144,512]{2,1,0:T(8,128)(2,1)S(1)}, u32[]{:S(2)}, u32[]{:S(2)}) collective-permute-start(bf16[8,144,512]{2,1,0:T(8,128)(2,1)S(1)} %fusion.22), channel_id=1, source_target_pairs={{0,16},{8,24},{16,0},{24,8},{1,17},{9,25},{17,1},{25,9},{2,18},{10... | collective-permute-start | bytes 3538952 | tf_op jit(solution)/shard_map/ppermute | solution.py:95
  56.4 51.0 %collective-permute-start.17 = (bf16[8,144,512]{2,1,0:T(8,128)(2,1)S(1)}, bf16[8,144,512]{2,1,0:T(8,128)(2,1)S(1)}, u32[]{:S(2)}, u32[]{:S(2)}) collective-permute-start(bf16[8,144,512]{2,1,0:T(8,128)(2,1)S(1)} %fusion.25), channel_id=1, source_target_pairs={{0,8},{8,0},{16,24},{24,16},{1,9},{9,1},{17,25},{25,17},{2,10},{10... | collective-permute-start | bytes 3538952 | tf_op jit(solution)/shard_map/ppermute | solution.py:95
  58.2 51.0 %collective-permute-start.19 = (bf16[8,144,512]{2,1,0:T(8,128)(2,1)S(1)}, bf16[8,144,512]{2,1,0:T(8,128)(2,1)S(1)}, u32[]{:S(2)}, u32[]{:S(2)}) collective-permute-start(bf16[8,144,512]{2,1,0:T(8,128)(2,1)S(1)} %fusion.28), channel_id=1, source_target_pairs={{0,16},{8,24},{16,0},{24,8},{1,17},{9,25},{17,1},{25,9},{2,18},{10... | collective-permute-start | bytes 3538952 | tf_op jit(solution)/shard_map/ppermute | solution.py:95
  82.9 38.9 %collective-permute-start.14 = (bf16[8,72,512]{2,1,0:T(8,128)(2,1)S(1)}, bf16[8,72,512]{2,1,0:T(8,128)(2,1)S(1)}, u32[]{:S(2)}, u32[]{:S(2)}) collective-permute-start(bf16[8,72,512]{2,1,0:T(8,128)(2,1)S(1)} %slice.286), channel_id=1, source_target_pairs={{0,16},{8,24},{16,0},{24,8},{1,17},{9,25},{17,1},{25,9},{2,18},{10... | collective-permute-start | bytes 1769480 | tf_op jit(solution)/shard_map/ppermute | solution.py:95
  84.8 37.0 %collective-permute-start.16 = (bf16[8,72,512]{2,1,0:T(8,128)(2,1)S(1)}, bf16[8,72,512]{2,1,0:T(8,128)(2,1)S(1)}, u32[]{:S(2)}, u32[]{:S(2)}) collective-permute-start(bf16[8,72,512]{2,1,0:T(8,128)(2,1)S(1)} %slice.285), channel_id=1, source_target_pairs={{0,8},{8,0},{16,24},{24,16},{1,9},{9,1},{17,25},{25,17},{2,10},{10... | collective-permute-start | bytes 1769480 | tf_op jit(solution)/shard_map/ppermute | solution.py:95
  108.2 26.3 %collective-permute-start.18 = (bf16[8,72,512]{2,1,0:T(8,128)(2,1)S(1)}, bf16[8,72,512]{2,1,0:T(8,128)(2,1)S(1)}, u32[]{:S(2)}, u32[]{:S(2)}) collective-permute-start(bf16[8,72,512]{2,1,0:T(8,128)(2,1)S(1)} %slice.284), channel_id=1, source_target_pairs={{0,16},{8,24},{16,0},{24,8},{1,17},{9,25},{17,1},{25,9},{2,18},{10... | collective-permute-start | bytes 1769480 | tf_op jit(solution)/shard_map/ppermute | solution.py:95
  110.1 24.4 %collective-permute-start.20 = (bf16[8,72,512]{2,1,0:T(8,128)(2,1)S(1)}, bf16[8,72,512]{2,1,0:T(8,128)(2,1)S(1)}, u32[]{:S(2)}, u32[]{:S(2)}) collective-permute-start(bf16[8,72,512]{2,1,0:T(8,128)(2,1)S(1)} %slice.283), channel_id=1, source_target_pairs={{0,8},{8,0},{16,24},{24,16},{1,9},{9,1},{17,25},{25,17},{2,10},{10... | collective-permute-start | bytes 1769480 | tf_op jit(solution)/shard_map/ppermute | solution.py:95
  122.3 24.8 %collective-permute-start.21 = (bf16[8,72,512]{2,1,0:T(8,128)(2,1)S(1)}, bf16[8,72,512]{2,1,0:T(8,128)(2,1)S(1)}, u32[]{:S(2)}, u32[]{:S(2)}) collective-permute-start(bf16[8,72,512]{2,1,0:T(8,128)(2,1)S(1)} %fusion.46), channel_id=1, source_target_pairs={{0,16},{8,24},{16,0},{24,8},{1,17},{9,25},{17,1},{25,9},{2,18},{10... | collective-permute-start | bytes 1769480 | tf_op jit(solution)/shard_map/ppermute | solution.py:95
  123.0 42.4 %collective-permute-start.28 = (bf16[8,72,512]{2,1,0:T(8,128)(2,1)S(1)}, bf16[8,72,512]{2,1,0:T(8,128)(2,1)}, u32[]{:S(2)}, u32[]{:S(2)}) collective-permute-start(bf16[8,72,512]{2,1,0:T(8,128)(2,1)S(1)} %fusion.46), channel_id=1, source_target_pairs={{0,8},{8,0},{16,24},{24,16},{1,9},{9,1},{17,25},{25,17},{2,10},{10... | collective-permute-start | bytes 1769480 | tf_op jit(solution)/shard_map/ppermute | solution.py:95
  135.0 23.1 %collective-permute-start.22 = (bf16[8,72,512]{2,1,0:T(8,128)(2,1)S(1)}, bf16[8,72,512]{2,1,0:T(8,128)(2,1)}, u32[]{:S(2)}, u32[]{:S(2)}) collective-permute-start(bf16[8,72,512]{2,1,0:T(8,128)(2,1)S(1)} %fusion.44), channel_id=1, source_target_pairs={{0,16},{8,24},{16,0},{24,8},{1,17},{9,25},{17,1},{25,9},{2,18},{10... | collective-permute-start | bytes 1769480 | tf_op jit(solution)/shard_map/ppermute | solution.py:95
  135.6 33.7 %collective-permute-start.29 = (bf16[8,72,512]{2,1,0:T(8,128)(2,1)S(1)}, bf16[8,72,512]{2,1,0:T(8,128)(2,1)}, u32[]{:S(2)}, u32[]{:S(2)}) collective-permute-start(bf16[8,72,512]{2,1,0:T(8,128)(2,1)S(1)} %fusion.44), channel_id=1, source_target_pairs={{0,8},{8,0},{16,24},{24,16},{1,9},{9,1},{17,25},{25,17},{2,10},{10... | collective-permute-start | bytes 1769480 | tf_op jit(solution)/shard_map/ppermute | solution.py:95
  165.3 24.7 %collective-permute-start.23 = (bf16[4,128,512]{2,1,0:T(8,128)(2,1)}, bf16[4,128,512]{2,1,0:T(8,128)(2,1)S(1)}, u32[]{:S(2)}, u32[]{:S(2)}) collective-permute-start(bf16[4,128,512]{2,1,0:T(8,128)(2,1)} %bitcast.152), channel_id=1, source_target_pairs={{0,1},{1,0},{2,3},{3,2},{4,5},{5,4},{6,7},{7,6},{8,9},{9,8},{10,11... | collective-permute-start | bytes 1572872 | tf_op jit(solution)/shard_map/ppermute | solution.py:104
  166.3 14.5 %collective-permute-start.30 = (bf16[4,72,512]{2,1,0:T(8,128)(2,1)S(1)}, bf16[4,72,512]{2,1,0:T(8,128)(2,1)}, u32[]{:S(2)}, u32[]{:S(2)}) collective-permute-start(bf16[4,72,512]{2,1,0:T(8,128)(2,1)S(1)} %slice.194), channel_id=1, source_target_pairs={{0,16},{8,24},{16,0},{24,8},{1,17},{9,25},{17,1},{25,9},{2,18},{10... | collective-permute-start | bytes 884744 | tf_op jit(solution)/shard_map/ppermute | solution.py:95
  167.9 12.8 %collective-permute-start.31 = (bf16[4,72,512]{2,1,0:T(8,128)(2,1)S(1)}, bf16[4,72,512]{2,1,0:T(8,128)(2,1)}, u32[]{:S(2)}, u32[]{:S(2)}) collective-permute-start(bf16[4,72,512]{2,1,0:T(8,128)(2,1)S(1)} %slice.195), channel_id=1, source_target_pairs={{0,8},{8,0},{16,24},{24,16},{1,9},{9,1},{17,25},{25,17},{2,10},{10... | collective-permute-start | bytes 884744 | tf_op jit(solution)/shard_map/ppermute | solution.py:95
  170.3 11.9 %collective-permute-start.32 = (bf16[4,72,512]{2,1,0:T(8,128)(2,1)S(1)}, bf16[4,72,512]{2,1,0:T(8,128)(2,1)}, u32[]{:S(2)}, u32[]{:S(2)}) collective-permute-start(bf16[4,72,512]{2,1,0:T(8,128)(2,1)S(1)} %slice.196), channel_id=1, source_target_pairs={{0,16},{8,24},{16,0},{24,8},{1,17},{9,25},{17,1},{25,9},{2,18},{10... | collective-permute-start | bytes 884744 | tf_op jit(solution)/shard_map/ppermute | solution.py:95
  172.8 10.8 %collective-permute-start.33 = (bf16[4,72,512]{2,1,0:T(8,128)(2,1)S(1)}, bf16[4,72,512]{2,1,0:T(8,128)(2,1)}, u32[]{:S(2)}, u32[]{:S(2)}) collective-permute-start(bf16[4,72,512]{2,1,0:T(8,128)(2,1)S(1)} %slice.197), channel_id=1, source_target_pairs={{0,8},{8,0},{16,24},{24,16},{1,9},{9,1},{17,25},{25,17},{2,10},{10... | collective-permute-start | bytes 884744 | tf_op jit(solution)/shard_map/ppermute | solution.py:95
  190.2 7.9 %collective-permute-start.24 = (bf16[128,512]{1,0:T(8,128)(2,1)S(1)}, bf16[128,512]{1,0:T(8,128)(2,1)S(1)}, u32[]{:S(2)}, u32[]{:S(2)}) collective-permute-start(bf16[128,512]{1,0:T(8,128)(2,1)S(1)} %get-tuple-element.23), channel_id=1, source_target_pairs={{0,6},{2,0},{4,2},{6,4},{1,7},{3,1},{5,3},{7,5},{8,14},{10,8},{12,... | collective-permute-start | bytes 393224 | tf_op jit(solution)/shard_map/ppermute | solution.py:98
  192.9 12.9 %collective-permute-start.25 = (bf16[128,512]{1,0:T(8,128)(2,1)S(1)}, bf16[128,512]{1,0:T(8,128)(2,1)S(1)}, u32[]{:S(2)}, u32[]{:S(2)}) collective-permute-start(bf16[128,512]{1,0:T(8,128)(2,1)S(1)} %get-tuple-element.25), channel_id=1, source_target_pairs={{0,4},{2,6},{4,0},{6,2},{1,5},{3,7},{5,1},{7,3},{8,12},{10,14},{12... | collective-permute-start | bytes 393224 | tf_op jit(solution)/shard_map/ppermute | solution.py:98
  192.9 12.9 %collective-permute-start.26 = (bf16[128,512]{1,0:T(8,128)(2,1)S(1)}, bf16[128,512]{1,0:T(8,128)(2,1)S(1)}, u32[]{:S(2)}, u32[]{:S(2)}) collective-permute-start(bf16[128,512]{1,0:T(8,128)(2,1)S(1)} %get-tuple-element.24), channel_id=1, source_target_pairs={{0,2},{2,4},{4,6},{6,0},{1,3},{3,5},{5,7},{7,1},{8,10},{10,12},{12... | collective-permute-start | bytes 393224 | tf_op jit(solution)/shard_map/ppermute | solution.py:98
  193.7 12.8 %collective-permute-start.35 = (bf16[128,512]{1,0:T(8,128)(2,1)S(1)}, bf16[128,512]{1,0:T(8,128)(2,1)S(1)}, u32[]{:S(2)}, u32[]{:S(2)}) collective-permute-start(bf16[128,512]{1,0:T(8,128)(2,1)S(1)} %get-tuple-element.26), channel_id=1, source_target_pairs={{0,6},{2,0},{4,2},{6,4},{1,7},{3,1},{5,3},{7,5},{8,14},{10,8},{12,... | collective-permute-start | bytes 393224 | tf_op jit(solution)/shard_map/ppermute | solution.py:98
  197.0 19.3 %collective-permute-start.36 = (bf16[128,512]{1,0:T(8,128)(2,1)S(1)}, bf16[128,512]{1,0:T(8,128)(2,1)S(1)}, u32[]{:S(2)}, u32[]{:S(2)}) collective-permute-start(bf16[128,512]{1,0:T(8,128)(2,1)S(1)} %get-tuple-element.28), channel_id=1, source_target_pairs={{0,4},{2,6},{4,0},{6,2},{1,5},{3,7},{5,1},{7,3},{8,12},{10,14},{12... | collective-permute-start | bytes 393224 | tf_op jit(solution)/shard_map/ppermute | solution.py:98
  198.1 18.2 %collective-permute-start.37 = (bf16[128,512]{1,0:T(8,128)(2,1)S(1)}, bf16[128,512]{1,0:T(8,128)(2,1)S(1)}, u32[]{:S(2)}, u32[]{:S(2)}) collective-permute-start(bf16[128,512]{1,0:T(8,128)(2,1)S(1)} %get-tuple-element.27), channel_id=1, source_target_pairs={{0,2},{2,4},{4,6},{6,0},{1,3},{3,5},{5,7},{7,1},{8,10},{10,12},{12... | collective-permute-start | bytes 393224 | tf_op jit(solution)/shard_map/ppermute | solution.py:98
  205.9 11.7 %collective-permute-start.27 = (bf16[128,512]{1,0:T(8,128)(2,1)S(1)}, bf16[128,512]{1,0:T(8,128)(2,1)S(1)}, u32[]{:S(2)}, u32[]{:S(2)}) collective-permute-start(bf16[128,512]{1,0:T(8,128)(2,1)S(1)} %fusion.93), channel_id=1, source_target_pairs={{0,0},{1,16},{8,8},{9,24},{16,17},{17,1},{24,25},{25,9},{2,2},{3,1... | collective-permute-start | bytes 393224 | tf_op jit(solution)/shard_map/ppermute | solution.py:192
  (18 other events, 105.3 us)

commit v4 on v3

--- a/solution.py
+++ b/solution.py
@@ -113,12 +113,6 @@
         piece = lax.dynamic_slice_in_dim(mine, (me ^ j) * depth, depth, 1)
         sliced.append(piece if j == 0 else to_section(piece, j))
     sliced = jnp.stack(sliced)
-    half = jnp.stack([sliced if k == 0 else to_upper(sliced, k) for k in range(zs)], axis=1)
-    other = to_other_core(half)
-    rows = jnp.where(
-        first_core, jnp.stack([half, other], axis=2), jnp.stack([other, half], axis=2)
-    ).reshape(sections, sec_toks, depth)
-
     logits = jnp.dot(normed, router, preferred_element_type=jnp.float32)
     prob = jax.nn.sigmoid(logits)
     onehot_k = (routes[0][:, :, None] == jnp.arange(experts_all, dtype=jnp.int32)).astype(jnp.float32)
@@ -126,6 +120,12 @@
     gates = picked / jnp.sum(picked, axis=1, keepdims=True)
     table = jnp.concatenate([routes[0].astype(jnp.float32), gates], axis=1).T
     table = jnp.stack([table if j == 0 else to_section(table, j) for j in range(sections)])
+    sliced, table = lax.optimization_barrier((sliced, table))
+    half = jnp.stack([sliced if k == 0 else to_upper(sliced, k) for k in range(zs)], axis=1)
+    other = to_other_core(half)
+    rows = jnp.where(
+        first_core, jnp.stack([half, other], axis=2), jnp.stack([other, half], axis=2)
+    ).reshape(sections, sec_toks, depth)
     table = jnp.stack([table if k == 0 else to_upper(table, k) for k in range(zs)], axis=1)
     table = table.transpose(0, 1, 3, 2).reshape(sections, sec_toks, 2 * TOPK)
     all_routes, all_gates = table[..., :TOPK].astype(jnp.int32), table[..., TOPK:]

time: 224 us -> 226 us (level)
  transfers between devices with their start and end apart: 39 -> 39, of which waited for: 21 -> 21; matrix products, arithmetic and copies ran while one was open for 21% -> 20% of each run, Pallas kernels for 0% -> 0%
where the time goes in v4:
time: 226 us; the launch traced here: 225 us
  waiting for transfers between devices  122 us (54%)
  starting transfers between devices  45.8 us (20%)
  matrix products  37.6 us (17%)
  other arithmetic  13.3 us (6%)
  local copies, waits for them, and re-layouts  6.35 us (3%)
    ppermute x22, waiting for transfers between devices, to_section(): return lax.ppermute(x, 'section', [(s, s ^ j) for s in range(sections)])  82.5 us
    dot_general x4, matrix products, gated_sum(): jnp.einsum('ect,ecd->td', combine[j, lo:hi], out, preferred_element_type=...  27.8 us
    ppermute x22, starting transfers between devices, to_section(): return lax.ppermute(x, 'section', [(s, s ^ j) for s in range(sections)])  22.1 us
    ppermute x6, waiting for transfers between devices, to_lower(): return lax.ppermute(x, 'expert', [(i, (i - k) % zs) for i in range(zs)])  17.5 us
    ppermute x6, waiting for transfers between devices, to_upper(): return lax.ppermute(x, 'expert', [(i, (i + k) % zs) for i in range(zs)])  16.6 us
    ppermute x6, starting transfers between devices, to_upper(): return lax.ppermute(x, 'expert', [(i, (i + k) % zs) for i in range(zs)])  14.2 us
    ppermute x6, starting transfers between devices, to_lower(): return lax.ppermute(x, 'expert', [(i, (i - k) % zs) for i in range(zs)])  7.94 us
    dot_general x8, matrix products, product(): jnp.einsum('ecd,edh->ech', x, weight[lo:hi], preferred_element_type=jnp.f...  6.3 us
  transfers between devices with their start and end apart: 39, of which 21 were waited for; matrix products, arithmetic and copies ran while one was open for 20% of the time, Pallas kernels for 0%

profile of v4, /device:TPU:0, one launch (start us, length us, event | category | flops | bytes accessed | tf_op | source)
XLA Modules:
  0.0 225.4 jit_solution(3565663516454772702)
XLA Ops:
  0.0 1.6 multiply_reduce_fusion
  3.6 3.0 %collective-permute-start.3 = (f32[16,128]{1,0:T(8,128)S(1)}, f32[16,128]{1,0:T(8,128)S(1)}, u32[]{:S(2)}, u32[]{:S(2)}) collective-permute-start(f32[16,128]{1,0:T(8,128)S(1)} %get-tuple-element.40), channel_id=1, source_target_pairs={{0,8},{8,0},{16,24},{24,16},{1,9},{9,1},{17,25},{25,17},{2,10},{10... | collective-permute-start | bytes 24584 | tf_op jit(solution)/shard_map/ppermute | solution.py:95
  8.3 2.0 collective-permute-start
  12.7 2.5 %collective-permute-done.1 = bf16[64,512]{1,0:T(8,128)(2,1)S(1)} collective-permute-done((bf16[64,512]{1,0:T(8,128)(2,1)S(1)}, bf16[64,512]{1,0:T(8,128)(2,1)S(1)}, u32[]{:S(2)}, u32[]{:S(2)}) %collective-permute-start.1) | collective-permute-done | bytes 65568 | tf_op jit(solution)/shard_map/ppermute | solution.py:95
  15.2 1.8 collective-permute-done.2
  17.0 1.6 collective-permute-start.9
  18.7 2.6 %collective-permute-start.10 = (bf16[4,64,512]{2,1,0:T(8,128)(2,1)S(1)}, bf16[4,64,512]{2,1,0:T(8,128)(2,1)S(1)}, u32[]{:S(2)}, u32[]{:S(2)}) collective-permute-start(bf16[4,64,512]{2,1,0:T(8,128)(2,1)S(1)} %pad_maximum_fusion.25), channel_id=1, source_target_pairs={{0,4},{2,6},{4,0},{6,2},{1,5},{3,7},{5,1},{7,3},{8,12},{10,14},{12... | collective-permute-start | bytes 786440 | tf_op jit(solution)/shard_map/ppermute | solution.py:101
  22.6 5.6 %collective-permute-done.9 = bf16[4,64,512]{2,1,0:T(8,128)(2,1)S(1)} collective-permute-done((bf16[4,64,512]{2,1,0:T(8,128)(2,1)S(1)}, bf16[4,64,512]{2,1,0:T(8,128)(2,1)S(1)}, u32[]{:S(2)}, u32[]{:S(2)}) %collective-permute-start.9) | collective-permute-done | bytes 262176 | tf_op jit(solution)/shard_map/ppermute | solution.py:101
  28.2 8.0 %collective-permute-done.10 = bf16[4,64,512]{2,1,0:T(8,128)(2,1)S(1)} collective-permute-done((bf16[4,64,512]{2,1,0:T(8,128)(2,1)S(1)}, bf16[4,64,512]{2,1,0:T(8,128)(2,1)S(1)}, u32[]{:S(2)}, u32[]{:S(2)}) %collective-permute-start.10) | collective-permute-done | bytes 262176 | tf_op jit(solution)/shard_map/ppermute | solution.py:101
  36.4 6.1 %collective-permute-start.6 = (f32[4,16,128]{2,1,0:T(8,128)S(1)}, f32[4,16,128]{2,1,0:T(8,128)S(1)}, u32[]{:S(2)}, u32[]{:S(2)}) collective-permute-start(f32[4,16,128]{2,1,0:T(8,128)S(1)} %pad_maximum_fusion.26), channel_id=1, source_target_pairs={{0,2},{2,4},{4,6},{6,0},{1,3},{3,5},{5,7},{7,1},{8,10},{10,12},{12... | collective-permute-start | bytes 98312 | tf_op jit(solution)/shard_map/ppermute | solution.py:101
  42.5 1.6 collective-permute-start.7
  45.6 2.1 collective-permute-done.7
  49.1 1.9 maximum_select_fusion
  51.1 3.0 %fusion.18 = bf16[4,16,72,512]{3,2,1,0:T(8,128)(2,1)S(1)} fusion(bf16[4,512,512,1]{2,1,3,0:T(8,128)(2,1)S(1)} %bitcast.130, s32[4,16,512]{2,1,0:T(8,128)S(1)} %fusion.71), kind=kOutput, calls=%fused_computation.20 | convolution fusion | flops 2420637696 | bytes 6946816 | tf_op jit(solution)/shard_map/sect,std->secd/dot_general | solution.py:147
  60.4 1.7 collective-permute-start.19
  62.0 22.3 %collective-permute-done.13 = bf16[8,144,512]{2,1,0:T(8,128)(2,1)S(1)} collective-permute-done((bf16[8,144,512]{2,1,0:T(8,128)(2,1)S(1)}, bf16[8,144,512]{2,1,0:T(8,128)(2,1)S(1)}, u32[]{:S(2)}, u32[]{:S(2)}) %collective-permute-start.13) | collective-permute-done | bytes 1179680 | tf_op jit(solution)/shard_map/ppermute | solution.py:95
  88.2 21.4 %collective-permute-done.17 = bf16[8,144,512]{2,1,0:T(8,128)(2,1)S(1)} collective-permute-done((bf16[8,144,512]{2,1,0:T(8,128)(2,1)S(1)}, bf16[8,144,512]{2,1,0:T(8,128)(2,1)S(1)}, u32[]{:S(2)}, u32[]{:S(2)}) %collective-permute-start.17) | collective-permute-done | bytes 1179680 | tf_op jit(solution)/shard_map/ppermute | solution.py:95
  113.5 5.0 %select_convert_fusion = bf16[4,16,72,512]{3,2,1,0:T(8,128)(2,1)} fusion(bf16[4,16,512]{2,1,0:T(8,128)(2,1)S(1)} %fusion.75, s32[4,16,512]{2,1,0:T(8,128)S(1)} %fusion.71), kind=kLoop, calls=%fused_computation | loop fusion | flops 4718592 | bytes 4915200 | tf_op jit(solution)/shard_map/convert_element_type | solution.py:145
  118.5 5.6 %collective-permute-done.14 = bf16[8,72,512]{2,1,0:T(8,128)(2,1)S(1)} collective-permute-done((bf16[8,72,512]{2,1,0:T(8,128)(2,1)S(1)}, bf16[8,72,512]{2,1,0:T(8,128)(2,1)S(1)}, u32[]{:S(2)}, u32[]{:S(2)}) %collective-permute-start.14) | collective-permute-done | bytes 589856 | tf_op jit(solution)/shard_map/ppermute | solution.py:95
  126.1 10.7 %collective-permute-done.18 = bf16[8,72,512]{2,1,0:T(8,128)(2,1)S(1)} collective-permute-done((bf16[8,72,512]{2,1,0:T(8,128)(2,1)S(1)}, bf16[8,72,512]{2,1,0:T(8,128)(2,1)S(1)}, u32[]{:S(2)}, u32[]{:S(2)}) %collective-permute-start.18) | collective-permute-done | bytes 589856 | tf_op jit(solution)/shard_map/ppermute | solution.py:95
  138.7 7.0 %fusion.31 = bf16[512,512]{1,0:T(8,128)(2,1)} fusion(bf16[4,16,72,512]{3,2,1,0:T(8,128)(2,1)} %select_convert_fusion, bf16[16,512,512]{2,1,0:T(8,128)(2,1)} %param.16, bf16[8,72,512]{2,1,0:T(8,128)(2,1)S(1)} %fusion.44, bf16[8,72,512]{2,1,0:T(8,128)(2,1)S(1)} %fusion.46), kind=kOutput, calls=%fused_computation.48 | convolution fusion | flops 1209401344 | bytes 11272192 | tf_op jit(solution)/shard_map/ect,ecd->td/dot_general | solution.py:165
  145.8 3.7 %collective-permute-done.21 = bf16[8,72,512]{2,1,0:T(8,128)(2,1)S(1)} collective-permute-done((bf16[8,72,512]{2,1,0:T(8,128)(2,1)S(1)}, bf16[8,72,512]{2,1,0:T(8,128)(2,1)S(1)}, u32[]{:S(2)}, u32[]{:S(2)}) %collective-permute-start.21) | collective-permute-done | bytes 589856 | tf_op jit(solution)/shard_map/ppermute | solution.py:95
  150.2 10.0 %collective-permute-done.22 = bf16[8,72,512]{2,1,0:T(8,128)(2,1)} collective-permute-done((bf16[8,72,512]{2,1,0:T(8,128)(2,1)S(1)}, bf16[8,72,512]{2,1,0:T(8,128)(2,1)}, u32[]{:S(2)}, u32[]{:S(2)}) %collective-permute-start.22) | collective-permute-done | bytes 589856 | tf_op jit(solution)/shard_map/ppermute | solution.py:95
  160.3 7.2 %broadcast_select_fusion.2 = (bf16[512,512]{1,0:T(8,128)(2,1)}, bf16[512,512]{1,0:T(8,128)(2,1)S(1)}) fusion(bf16[512,512]{1,0:T(8,128)(2,1)} %fusion.31, pred[]{:T(512)S(6)} %eq.48, bf16[16,512,512]{2,1,0:T(8,128)(2,1)} %param.16, bf16[8,72,512]{2,1,0:T(8,128)(2,1)} %collective-permute-done.22, bf16[8,72,512]{2,1,0:T(8,128)(2,1)} %copy-done.2, ...), kind=kOutput, calls=%fused_computation.120 | convolution fusion | flops 1209925632 | bytes 12320769 | tf_op jit(solution)/shard_map/ect,ecd->td/dot_general | solution.py:165
  171.6 1.8 collective-permute-start.32
  175.7 7.2 %fusion.33 = bf16[512,512]{1,0:T(8,128)(2,1)} fusion(bf16[4,16,72,512]{3,2,1,0:T(8,128)(2,1)} %select_convert_fusion, bf16[16,512,512]{2,1,0:T(8,128)(2,1)} %param.16, bf16[8,72,512]{2,1,0:T(8,128)(2,1)} %collective-permute-done.29, bf16[8,72,512]{2,1,0:T(8,128)(2,1)} %collective-permute-done.28), kind=kOutput, calls=%fused_computation.50 | convolution fusion | flops 1209401344 | bytes 11272192 | tf_op jit(solution)/shard_map/ect,ecd->td/dot_general | solution.py:165
  185.4 6.4 %broadcast_select_fusion = (bf16[512,512]{1,0:T(8,128)(2,1)S(1)}, bf16[512,512]{1,0:T(8,128)(2,1)S(1)}) fusion(bf16[512,512]{1,0:T(8,128)(2,1)} %fusion.33, pred[]{:T(512)S(6)} %eq.48, bf16[16,512,512]{2,1,0:T(8,128)(2,1)} %param.16, bf16[4,72,512]{2,1,0:T(8,128)(2,1)} %collective-permute-done.33, bf16[4,72,512]{2,1,0:T(8,128)(2,1)} %collective-permute-done.32, ...), kind=kOutput, calls=%fused_computation.118 | convolution fusion | flops 1211105280 | bytes 12320769 | tf_op jit(solution)/shard_map/ect,ecd->td/dot_general | solution.py:165
  192.1 2.9 %collective-permute-start.24 = (bf16[128,512]{1,0:T(8,128)(2,1)S(1)}, bf16[128,512]{1,0:T(8,128)(2,1)S(1)}, u32[]{:S(2)}, u32[]{:S(2)}) collective-permute-start(bf16[128,512]{1,0:T(8,128)(2,1)S(1)} %get-tuple-element.27), channel_id=1, source_target_pairs={{0,6},{2,0},{4,2},{6,4},{1,7},{3,1},{5,3},{7,5},{8,14},{10,8},{12,... | collective-permute-start | bytes 393224 | tf_op jit(solution)/shard_map/ppermute | solution.py:98
  195.9 3.2 %collective-permute-start.35 = (bf16[128,512]{1,0:T(8,128)(2,1)S(1)}, bf16[128,512]{1,0:T(8,128)(2,1)S(1)}, u32[]{:S(2)}, u32[]{:S(2)}) collective-permute-start(bf16[128,512]{1,0:T(8,128)(2,1)S(1)} %get-tuple-element.30), channel_id=1, source_target_pairs={{0,6},{2,0},{4,2},{6,4},{1,7},{3,1},{5,3},{7,5},{8,14},{10,8},{12,... | collective-permute-start | bytes 393224 | tf_op jit(solution)/shard_map/ppermute | solution.py:98
  200.2 7.7 %collective-permute-done.25 = bf16[128,512]{1,0:T(8,128)(2,1)S(1)} collective-permute-done((bf16[128,512]{1,0:T(8,128)(2,1)S(1)}, bf16[128,512]{1,0:T(8,128)(2,1)S(1)}, u32[]{:S(2)}, u32[]{:S(2)}) %collective-permute-start.25) | collective-permute-done | bytes 131104 | tf_op jit(solution)/shard_map/ppermute | solution.py:98
  208.7 9.8 %collective-permute-done.36 = bf16[128,512]{1,0:T(8,128)(2,1)S(1)} collective-permute-done((bf16[128,512]{1,0:T(8,128)(2,1)S(1)}, bf16[128,512]{1,0:T(8,128)(2,1)S(1)}, u32[]{:S(2)}, u32[]{:S(2)}) %collective-permute-start.36) | collective-permute-done | bytes 131104 | tf_op jit(solution)/shard_map/ppermute | solution.py:98
  219.3 5.3 %collective-permute-done.38 = bf16[128,512]{1,0:T(8,128)(2,1)S(1)} collective-permute-done((bf16[128,512]{1,0:T(8,128)(2,1)S(1)}, bf16[128,512]{1,0:T(8,128)(2,1)S(1)}, u32[]{:S(2)}, u32[]{:S(2)}) %collective-permute-start.38) | collective-permute-done | bytes 131104 | tf_op jit(solution)/shard_map/ppermute | solution.py:192
  (115 shorter events, 42.6 us)
Async XLA Ops:
  3.6 8.3 %collective-permute-start.3 = (f32[16,128]{1,0:T(8,128)S(1)}, f32[16,128]{1,0:T(8,128)S(1)}, u32[]{:S(2)}, u32[]{:S(2)}) collective-permute-start(f32[16,128]{1,0:T(8,128)S(1)} %get-tuple-element.40), channel_id=1, source_target_pairs={{0,8},{8,0},{16,24},{24,16},{1,9},{9,1},{17,25},{25,17},{2,10},{10... | collective-permute-start | bytes 24584 | tf_op jit(solution)/shard_map/ppermute | solution.py:95
  6.6 5.3 %collective-permute-start.4 = (f32[16,128]{1,0:T(8,128)S(1)}, f32[16,128]{1,0:T(8,128)S(1)}, u32[]{:S(2)}, u32[]{:S(2)}) collective-permute-start(f32[16,128]{1,0:T(8,128)S(1)} %get-tuple-element.40), channel_id=1, source_target_pairs={{0,16},{8,24},{16,0},{24,8},{1,17},{9,25},{17,1},{25,9},{2,18},{10... | collective-permute-start | bytes 24584 | tf_op jit(solution)/shard_map/ppermute | solution.py:95
  17.0 11.2 %collective-permute-start.9 = (bf16[4,64,512]{2,1,0:T(8,128)(2,1)S(1)}, bf16[4,64,512]{2,1,0:T(8,128)(2,1)S(1)}, u32[]{:S(2)}, u32[]{:S(2)}) collective-permute-start(bf16[4,64,512]{2,1,0:T(8,128)(2,1)S(1)} %pad_maximum_fusion.25), channel_id=1, source_target_pairs={{0,2},{2,4},{4,6},{6,0},{1,3},{3,5},{5,7},{7,1},{8,10},{10,12},{12... | collective-permute-start | bytes 786440 | tf_op jit(solution)/shard_map/ppermute | solution.py:101
  18.7 17.5 %collective-permute-start.10 = (bf16[4,64,512]{2,1,0:T(8,128)(2,1)S(1)}, bf16[4,64,512]{2,1,0:T(8,128)(2,1)S(1)}, u32[]{:S(2)}, u32[]{:S(2)}) collective-permute-start(bf16[4,64,512]{2,1,0:T(8,128)(2,1)S(1)} %pad_maximum_fusion.25), channel_id=1, source_target_pairs={{0,4},{2,6},{4,0},{6,2},{1,5},{3,7},{5,1},{7,3},{8,12},{10,14},{12... | collective-permute-start | bytes 786440 | tf_op jit(solution)/shard_map/ppermute | solution.py:101
  21.2 14.9 %collective-permute-start.11 = (bf16[4,64,512]{2,1,0:T(8,128)(2,1)S(1)}, bf16[4,64,512]{2,1,0:T(8,128)(2,1)S(1)}, u32[]{:S(2)}, u32[]{:S(2)}) collective-permute-start(bf16[4,64,512]{2,1,0:T(8,128)(2,1)S(1)} %pad_maximum_fusion.25), channel_id=1, source_target_pairs={{0,6},{2,0},{4,2},{6,4},{1,7},{3,1},{5,3},{7,5},{8,14},{10,8},{12,... | collective-permute-start | bytes 786440 | tf_op jit(solution)/shard_map/ppermute | solution.py:101
  36.3 12.8 %collective-permute-start.12 = (bf16[4,4,64,512]{3,2,1,0:T(8,128)(2,1)S(1)}, bf16[4,4,64,512]{3,2,1,0:T(8,128)(2,1)}, u32[]{:S(2)}, u32[]{:S(2)}) collective-permute-start(bf16[4,4,64,512]{3,2,1,0:T(8,128)(2,1)S(1)} %get-tuple-element.26), channel_id=1, source_target_pairs={{0,1},{1,0},{2,3},{3,2},{4,5},{5,4},{6,7},{7,6},{8,9},{9,8},{10,11... | collective-permute-start | bytes 3145736 | tf_op jit(solution)/shard_map/ppermute | solution.py:104
  36.4 9.2 %collective-permute-start.6 = (f32[4,16,128]{2,1,0:T(8,128)S(1)}, f32[4,16,128]{2,1,0:T(8,128)S(1)}, u32[]{:S(2)}, u32[]{:S(2)}) collective-permute-start(f32[4,16,128]{2,1,0:T(8,128)S(1)} %pad_maximum_fusion.26), channel_id=1, source_target_pairs={{0,2},{2,4},{4,6},{6,0},{1,3},{3,5},{5,7},{7,1},{8,10},{10,12},{12... | collective-permute-start | bytes 98312 | tf_op jit(solution)/shard_map/ppermute | solution.py:101
  55.4 29.0 %collective-permute-start.13 = (bf16[8,144,512]{2,1,0:T(8,128)(2,1)S(1)}, bf16[8,144,512]{2,1,0:T(8,128)(2,1)S(1)}, u32[]{:S(2)}, u32[]{:S(2)}) collective-permute-start(bf16[8,144,512]{2,1,0:T(8,128)(2,1)S(1)} %fusion.19), channel_id=1, source_target_pairs={{0,8},{8,0},{16,24},{24,16},{1,9},{9,1},{17,25},{25,17},{2,10},{10... | collective-permute-start | bytes 3538952 | tf_op jit(solution)/shard_map/ppermute | solution.py:95
  57.3 29.0 %collective-permute-start.15 = (bf16[8,144,512]{2,1,0:T(8,128)(2,1)S(1)}, bf16[8,144,512]{2,1,0:T(8,128)(2,1)S(1)}, u32[]{:S(2)}, u32[]{:S(2)}) collective-permute-start(bf16[8,144,512]{2,1,0:T(8,128)(2,1)S(1)} %fusion.22), channel_id=1, source_target_pairs={{0,16},{8,24},{16,0},{24,8},{1,17},{9,25},{17,1},{25,9},{2,18},{10... | collective-permute-start | bytes 3538952 | tf_op jit(solution)/shard_map/ppermute | solution.py:95
  58.5 51.1 %collective-permute-start.17 = (bf16[8,144,512]{2,1,0:T(8,128)(2,1)S(1)}, bf16[8,144,512]{2,1,0:T(8,128)(2,1)S(1)}, u32[]{:S(2)}, u32[]{:S(2)}) collective-permute-start(bf16[8,144,512]{2,1,0:T(8,128)(2,1)S(1)} %fusion.25), channel_id=1, source_target_pairs={{0,8},{8,0},{16,24},{24,16},{1,9},{9,1},{17,25},{25,17},{2,10},{10... | collective-permute-start | bytes 3538952 | tf_op jit(solution)/shard_map/ppermute | solution.py:95
  60.4 51.1 %collective-permute-start.19 = (bf16[8,144,512]{2,1,0:T(8,128)(2,1)S(1)}, bf16[8,144,512]{2,1,0:T(8,128)(2,1)S(1)}, u32[]{:S(2)}, u32[]{:S(2)}) collective-permute-start(bf16[8,144,512]{2,1,0:T(8,128)(2,1)S(1)} %fusion.28), channel_id=1, source_target_pairs={{0,16},{8,24},{16,0},{24,8},{1,17},{9,25},{17,1},{25,9},{2,18},{10... | collective-permute-start | bytes 3538952 | tf_op jit(solution)/shard_map/ppermute | solution.py:95
  85.2 38.9 %collective-permute-start.14 = (bf16[8,72,512]{2,1,0:T(8,128)(2,1)S(1)}, bf16[8,72,512]{2,1,0:T(8,128)(2,1)S(1)}, u32[]{:S(2)}, u32[]{:S(2)}) collective-permute-start(bf16[8,72,512]{2,1,0:T(8,128)(2,1)S(1)} %slice.286), channel_id=1, source_target_pairs={{0,16},{8,24},{16,0},{24,8},{1,17},{9,25},{17,1},{25,9},{2,18},{10... | collective-permute-start | bytes 1769480 | tf_op jit(solution)/shard_map/ppermute | solution.py:95
  87.1 37.0 %collective-permute-start.16 = (bf16[8,72,512]{2,1,0:T(8,128)(2,1)S(1)}, bf16[8,72,512]{2,1,0:T(8,128)(2,1)S(1)}, u32[]{:S(2)}, u32[]{:S(2)}) collective-permute-start(bf16[8,72,512]{2,1,0:T(8,128)(2,1)S(1)} %slice.285), channel_id=1, source_target_pairs={{0,8},{8,0},{16,24},{24,16},{1,9},{9,1},{17,25},{25,17},{2,10},{10... | collective-permute-start | bytes 1769480 | tf_op jit(solution)/shard_map/ppermute | solution.py:95
  110.5 26.3 %collective-permute-start.18 = (bf16[8,72,512]{2,1,0:T(8,128)(2,1)S(1)}, bf16[8,72,512]{2,1,0:T(8,128)(2,1)S(1)}, u32[]{:S(2)}, u32[]{:S(2)}) collective-permute-start(bf16[8,72,512]{2,1,0:T(8,128)(2,1)S(1)} %slice.284), channel_id=1, source_target_pairs={{0,16},{8,24},{16,0},{24,8},{1,17},{9,25},{17,1},{25,9},{2,18},{10... | collective-permute-start | bytes 1769480 | tf_op jit(solution)/shard_map/ppermute | solution.py:95
  112.4 24.4 %collective-permute-start.20 = (bf16[8,72,512]{2,1,0:T(8,128)(2,1)S(1)}, bf16[8,72,512]{2,1,0:T(8,128)(2,1)S(1)}, u32[]{:S(2)}, u32[]{:S(2)}) collective-permute-start(bf16[8,72,512]{2,1,0:T(8,128)(2,1)S(1)} %slice.283), channel_id=1, source_target_pairs={{0,8},{8,0},{16,24},{24,16},{1,9},{9,1},{17,25},{25,17},{2,10},{10... | collective-permute-start | bytes 1769480 | tf_op jit(solution)/shard_map/ppermute | solution.py:95
  124.6 24.8 %collective-permute-start.21 = (bf16[8,72,512]{2,1,0:T(8,128)(2,1)S(1)}, bf16[8,72,512]{2,1,0:T(8,128)(2,1)S(1)}, u32[]{:S(2)}, u32[]{:S(2)}) collective-permute-start(bf16[8,72,512]{2,1,0:T(8,128)(2,1)S(1)} %fusion.46), channel_id=1, source_target_pairs={{0,16},{8,24},{16,0},{24,8},{1,17},{9,25},{17,1},{25,9},{2,18},{10... | collective-permute-start | bytes 1769480 | tf_op jit(solution)/shard_map/ppermute | solution.py:95
  125.1 42.4 %collective-permute-start.28 = (bf16[8,72,512]{2,1,0:T(8,128)(2,1)S(1)}, bf16[8,72,512]{2,1,0:T(8,128)(2,1)}, u32[]{:S(2)}, u32[]{:S(2)}) collective-permute-start(bf16[8,72,512]{2,1,0:T(8,128)(2,1)S(1)} %fusion.46), channel_id=1, source_target_pairs={{0,8},{8,0},{16,24},{24,16},{1,9},{9,1},{17,25},{25,17},{2,10},{10... | collective-permute-start | bytes 1769480 | tf_op jit(solution)/shard_map/ppermute | solution.py:95
  137.3 23.0 %collective-permute-start.22 = (bf16[8,72,512]{2,1,0:T(8,128)(2,1)S(1)}, bf16[8,72,512]{2,1,0:T(8,128)(2,1)}, u32[]{:S(2)}, u32[]{:S(2)}) collective-permute-start(bf16[8,72,512]{2,1,0:T(8,128)(2,1)S(1)} %fusion.44), channel_id=1, source_target_pairs={{0,16},{8,24},{16,0},{24,8},{1,17},{9,25},{17,1},{25,9},{2,18},{10... | collective-permute-start | bytes 1769480 | tf_op jit(solution)/shard_map/ppermute | solution.py:95
  137.7 32.9 %collective-permute-start.29 = (bf16[8,72,512]{2,1,0:T(8,128)(2,1)S(1)}, bf16[8,72,512]{2,1,0:T(8,128)(2,1)}, u32[]{:S(2)}, u32[]{:S(2)}) collective-permute-start(bf16[8,72,512]{2,1,0:T(8,128)(2,1)S(1)} %fusion.44), channel_id=1, source_target_pairs={{0,8},{8,0},{16,24},{24,16},{1,9},{9,1},{17,25},{25,17},{2,10},{10... | collective-permute-start | bytes 1769480 | tf_op jit(solution)/shard_map/ppermute | solution.py:95
  167.5 24.5 %collective-permute-start.23 = (bf16[4,128,512]{2,1,0:T(8,128)(2,1)}, bf16[4,128,512]{2,1,0:T(8,128)(2,1)S(1)}, u32[]{:S(2)}, u32[]{:S(2)}) collective-permute-start(bf16[4,128,512]{2,1,0:T(8,128)(2,1)} %bitcast.152), channel_id=1, source_target_pairs={{0,1},{1,0},{2,3},{3,2},{4,5},{5,4},{6,7},{7,6},{8,9},{9,8},{10,11... | collective-permute-start | bytes 1572872 | tf_op jit(solution)/shard_map/ppermute | solution.py:104
  168.5 14.4 %collective-permute-start.30 = (bf16[4,72,512]{2,1,0:T(8,128)(2,1)S(1)}, bf16[4,72,512]{2,1,0:T(8,128)(2,1)}, u32[]{:S(2)}, u32[]{:S(2)}) collective-permute-start(bf16[4,72,512]{2,1,0:T(8,128)(2,1)S(1)} %slice.194), channel_id=1, source_target_pairs={{0,16},{8,24},{16,0},{24,8},{1,17},{9,25},{17,1},{25,9},{2,18},{10... | collective-permute-start | bytes 884744 | tf_op jit(solution)/shard_map/ppermute | solution.py:95
  169.8 13.1 %collective-permute-start.31 = (bf16[4,72,512]{2,1,0:T(8,128)(2,1)S(1)}, bf16[4,72,512]{2,1,0:T(8,128)(2,1)}, u32[]{:S(2)}, u32[]{:S(2)}) collective-permute-start(bf16[4,72,512]{2,1,0:T(8,128)(2,1)S(1)} %slice.195), channel_id=1, source_target_pairs={{0,8},{8,0},{16,24},{24,16},{1,9},{9,1},{17,25},{25,17},{2,10},{10... | collective-permute-start | bytes 884744 | tf_op jit(solution)/shard_map/ppermute | solution.py:95
  171.6 12.8 %collective-permute-start.32 = (bf16[4,72,512]{2,1,0:T(8,128)(2,1)S(1)}, bf16[4,72,512]{2,1,0:T(8,128)(2,1)}, u32[]{:S(2)}, u32[]{:S(2)}) collective-permute-start(bf16[4,72,512]{2,1,0:T(8,128)(2,1)S(1)} %slice.196), channel_id=1, source_target_pairs={{0,16},{8,24},{16,0},{24,8},{1,17},{9,25},{17,1},{25,9},{2,18},{10... | collective-permute-start | bytes 884744 | tf_op jit(solution)/shard_map/ppermute | solution.py:95
  174.4 11.1 %collective-permute-start.33 = (bf16[4,72,512]{2,1,0:T(8,128)(2,1)S(1)}, bf16[4,72,512]{2,1,0:T(8,128)(2,1)}, u32[]{:S(2)}, u32[]{:S(2)}) collective-permute-start(bf16[4,72,512]{2,1,0:T(8,128)(2,1)S(1)} %slice.197), channel_id=1, source_target_pairs={{0,8},{8,0},{16,24},{24,16},{1,9},{9,1},{17,25},{25,17},{2,10},{10... | collective-permute-start | bytes 884744 | tf_op jit(solution)/shard_map/ppermute | solution.py:95
  192.1 8.1 %collective-permute-start.24 = (bf16[128,512]{1,0:T(8,128)(2,1)S(1)}, bf16[128,512]{1,0:T(8,128)(2,1)S(1)}, u32[]{:S(2)}, u32[]{:S(2)}) collective-permute-start(bf16[128,512]{1,0:T(8,128)(2,1)S(1)} %get-tuple-element.27), channel_id=1, source_target_pairs={{0,6},{2,0},{4,2},{6,4},{1,7},{3,1},{5,3},{7,5},{8,14},{10,8},{12,... | collective-permute-start | bytes 393224 | tf_op jit(solution)/shard_map/ppermute | solution.py:98
  195.0 12.9 %collective-permute-start.25 = (bf16[128,512]{1,0:T(8,128)(2,1)S(1)}, bf16[128,512]{1,0:T(8,128)(2,1)S(1)}, u32[]{:S(2)}, u32[]{:S(2)}) collective-permute-start(bf16[128,512]{1,0:T(8,128)(2,1)S(1)} %get-tuple-element.29), channel_id=1, source_target_pairs={{0,4},{2,6},{4,0},{6,2},{1,5},{3,7},{5,1},{7,3},{8,12},{10,14},{12... | collective-permute-start | bytes 393224 | tf_op jit(solution)/shard_map/ppermute | solution.py:98
  195.0 12.9 %collective-permute-start.26 = (bf16[128,512]{1,0:T(8,128)(2,1)S(1)}, bf16[128,512]{1,0:T(8,128)(2,1)S(1)}, u32[]{:S(2)}, u32[]{:S(2)}) collective-permute-start(bf16[128,512]{1,0:T(8,128)(2,1)S(1)} %get-tuple-element.28), channel_id=1, source_target_pairs={{0,2},{2,4},{4,6},{6,0},{1,3},{3,5},{5,7},{7,1},{8,10},{10,12},{12... | collective-permute-start | bytes 393224 | tf_op jit(solution)/shard_map/ppermute | solution.py:98
  195.9 12.8 %collective-permute-start.35 = (bf16[128,512]{1,0:T(8,128)(2,1)S(1)}, bf16[128,512]{1,0:T(8,128)(2,1)S(1)}, u32[]{:S(2)}, u32[]{:S(2)}) collective-permute-start(bf16[128,512]{1,0:T(8,128)(2,1)S(1)} %get-tuple-element.30), channel_id=1, source_target_pairs={{0,6},{2,0},{4,2},{6,4},{1,7},{3,1},{5,3},{7,5},{8,14},{10,8},{12,... | collective-permute-start | bytes 393224 | tf_op jit(solution)/shard_map/ppermute | solution.py:98
  199.1 19.3 %collective-permute-start.36 = (bf16[128,512]{1,0:T(8,128)(2,1)S(1)}, bf16[128,512]{1,0:T(8,128)(2,1)S(1)}, u32[]{:S(2)}, u32[]{:S(2)}) collective-permute-start(bf16[128,512]{1,0:T(8,128)(2,1)S(1)} %get-tuple-element.32), channel_id=1, source_target_pairs={{0,4},{2,6},{4,0},{6,2},{1,5},{3,7},{5,1},{7,3},{8,12},{10,14},{12... | collective-permute-start | bytes 393224 | tf_op jit(solution)/shard_map/ppermute | solution.py:98
  200.2 18.2 %collective-permute-start.37 = (bf16[128,512]{1,0:T(8,128)(2,1)S(1)}, bf16[128,512]{1,0:T(8,128)(2,1)S(1)}, u32[]{:S(2)}, u32[]{:S(2)}) collective-permute-start(bf16[128,512]{1,0:T(8,128)(2,1)S(1)} %get-tuple-element.31), channel_id=1, source_target_pairs={{0,2},{2,4},{4,6},{6,0},{1,3},{3,5},{5,7},{7,1},{8,10},{10,12},{12... | collective-permute-start | bytes 393224 | tf_op jit(solution)/shard_map/ppermute | solution.py:98
  208.0 11.3 %collective-permute-start.27 = (bf16[128,512]{1,0:T(8,128)(2,1)S(1)}, bf16[128,512]{1,0:T(8,128)(2,1)S(1)}, u32[]{:S(2)}, u32[]{:S(2)}) collective-permute-start(bf16[128,512]{1,0:T(8,128)(2,1)S(1)} %fusion.93), channel_id=1, source_target_pairs={{0,0},{1,16},{8,8},{9,24},{16,17},{17,1},{24,25},{25,9},{2,2},{3,1... | collective-permute-start | bytes 393224 | tf_op jit(solution)/shard_map/ppermute | solution.py:192
  218.5 6.1 %collective-permute-start.38 = (bf16[128,512]{1,0:T(8,128)(2,1)S(1)}, bf16[128,512]{1,0:T(8,128)(2,1)S(1)}, u32[]{:S(2)}, u32[]{:S(2)}) collective-permute-start(bf16[128,512]{1,0:T(8,128)(2,1)S(1)} %fusion.90), channel_id=1, source_target_pairs={{0,8},{1,24},{8,0},{9,16},{16,25},{17,9},{24,17},{25,1},{2,10},{3,... | collective-permute-start | bytes 393224 | tf_op jit(solution)/shard_map/ppermute | solution.py:192
  (15 other events, 84.9 us)
